TPU v7x, 256 devices: a whole 4x4x8 slice. The times are simulated.
256 devices in a mesh: head: 4 (over z_lo, core), inner: 4 (over z_hi), outer: 16 (over y, x).
Axes of the slice: x: 4, y: 4, z: 8 (z_hi: 4, z_lo: 2; z = z_hi * 2 + z_lo), core: 2. Of those that a mesh axis runs over, the one named last changes fastest.
Arguments:
- query: bfloat16 [64, 192, 16, 128], P(('inner', 'outer'), 'head'), may hold values from -8 to 8
- key_in: bfloat16 [64, 192, 16, 128], P(('inner', 'outer'), 'head'), may hold values from -8 to 8
- value: bfloat16 [64, 192, 16, 128], P(('inner', 'outer'), 'head'), may hold values from -6 to 6
- doc_ids: int32 [12288], P(('inner', 'outer')), may hold values from 0 to 7, never falling along the last dimension, each value on 1 to 6144 neighbouring positions
- out_weight: bfloat16 [2048, 4096], P('head'), may hold values from -0.25 to 0.25
Outputs:
- mixed: bfloat16 [64, 192, 4096], P(('inner', 'outer'), 'head')
Inputs may be any that keep to these rules, and one draw needn't show every extreme that they name: `doc_ids`: record numbers never fall along the tokens; a record may span up to 6144 positions.
All inputs are finite; a program needn't handle non-finite values.
Results may differ from a plain program's by a relative error of at most 0.012.
Values may be sent and summed in bfloat16 or wider, within the bound.
No kernel may reach another device: no remote copies, remote signals or barrier semaphores. Data moves between devices by JAX's collectives and lax.ppermute only.
A program may use at most 192 MiB of HBM per device.

v0:
```python
import math

import jax
import jax.numpy as jnp
from jax import lax
from jax.sharding import PartitionSpec as P


def online_update(running, queries, key_block, value_block, allowed, scaling):
    running_max, running_sum, accumulated = running
    scores = (
        jnp.einsum("qhd,khd->hqk", queries, key_block, preferred_element_type=jnp.float32) * scaling
    )
    scores = jnp.where(allowed[None], scores, -jnp.inf)
    new_max = jnp.maximum(running_max, jnp.max(scores, axis=-1))
    weights = jnp.exp(scores - new_max[..., None])
    new_sum = jnp.sum(weights, axis=-1)
    product = jnp.einsum(
        "hqk,khd->hqd",
        weights.astype(jnp.bfloat16),
        value_block,
        preferred_element_type=jnp.float32,
    )
    return (new_max, new_sum, product)


def fold_block(running, pieces, positions, queries, query_pos, query_doc, scaling):
    key_block, value_block, doc_block = pieces
    allowed = (positions[None, :] <= query_pos[:, None]) & (
        doc_block[None, :] == query_doc[:, None]
    )
    return online_update(running, queries, key_block, value_block, allowed, scaling)


def body(query, key_in, value, doc_ids, out_weight):
    local_rows = query.shape[1]
    head_count = query.shape[2]
    head_dim = query.shape[3]
    queries, keys_all, values_all = (
        lax.all_to_all(
            query.reshape(local_rows, head_count, head_dim),
            "head",
            split_axis=1,
            concat_axis=0,
            tiled=True,
        ),
        lax.all_to_all(
            key_in.reshape(local_rows, head_count, head_dim),
            "head",
            split_axis=1,
            concat_axis=0,
            tiled=True,
        ),
        lax.all_to_all(
            value.reshape(local_rows, head_count, head_dim),
            "head",
            split_axis=1,
            concat_axis=0,
            tiled=True,
        ),
    )
    block_rows = queries.shape[0]
    local_heads = queries.shape[1]
    block_start = lax.axis_index(("inner", "outer")) * block_rows
    query_pos = block_start + jnp.arange(block_rows, dtype=jnp.int32)
    scaling = 1.0 / math.sqrt(head_dim)
    initial = (
        jnp.full((local_heads, block_rows), -1e30, jnp.float32),
        jnp.zeros((local_heads, block_rows), jnp.float32),
        jnp.zeros((local_heads, block_rows, head_dim), jnp.float32),
    )
    pieces = (
        lax.all_gather(keys_all, ("inner", "outer"), axis=0, tiled=True),
        lax.all_gather(values_all, ("inner", "outer"), axis=0, tiled=True),
        lax.all_gather(doc_ids, ("inner", "outer"), axis=0, tiled=True),
    )
    positions = jnp.arange(pieces[0].shape[0], dtype=jnp.int32)
    finished = fold_block(initial, pieces, positions, queries, query_pos, doc_ids, scaling)
    running_max, running_sum, accumulated = finished
    attended = (accumulated / running_sum[..., None]).astype(jnp.bfloat16)
    attended = attended.transpose(1, 0, 2).reshape(block_rows, local_heads * head_dim)
    share_rows = block_rows // lax.axis_size("head")
    summed = lax.psum_scatter(
        jnp.dot(attended, out_weight, preferred_element_type=jnp.float32).astype(jnp.bfloat16),
        "head",
        scatter_dimension=0,
        tiled=True,
    ).astype(jnp.float32)
    return summed.astype(jnp.bfloat16).reshape(1, share_rows, summed.shape[1])


def solution(mesh):
    in_specs = (
        P(("inner", "outer"), "head", None, None),
        P(("inner", "outer"), "head", None, None),
        P(("inner", "outer"), "head", None, None),
        P(("inner", "outer")),
        P("head", None),
    )
    out_specs = P(("inner", "outer"), "head", None)
    return jax.shard_map(body, mesh=mesh, in_specs=in_specs, out_specs=out_specs, check_vma=False)
```

profile of v0, /device:TPU:1, one launch (start us, length us, event | category | flops | bytes accessed | tf_op | source)
XLA Modules:
  0.0 525.8 jit_solution(14583974250277232946)
XLA Ops:
  6.5 0.0 all-gather.3.cloned.1.call-start
  6.5 1.0 copy.29
  7.5 10.2 %all_to_all.54 = bf16[48,16,128]{2,0,1:T(8,128)(2,1)S(1)} all-to-all(bf16[48,16,128]{2,0,1:T(8,128)(2,1)S(1)} %bitcast.47), channel_id=1, replica_groups=mesh['head'=4,'inner'=4,'outer'=16] {'head'}, dimensions={1} | all-to-all | bytes 393216 | tf_op jit(solution)/shard_map/all_to_all | solution.py:47
  17.7 0.7 copy.16
  18.4 0.0 all-gather.3.cloned.1.call-update
  18.4 0.0 all-gather.5.cloned.1.call-start
  18.5 1.0 copy.28
  19.5 7.7 %all_to_all.55 = bf16[48,16,128]{2,0,1:T(8,128)(2,1)S(1)} all-to-all(bf16[48,16,128]{2,0,1:T(8,128)(2,1)S(1)} %bitcast.48), channel_id=1, replica_groups=mesh['head'=4,'inner'=4,'outer'=16] {'head'}, dimensions={1} | all-to-all | bytes 393216 | tf_op jit(solution)/shard_map/all_to_all | solution.py:54
  27.2 0.7 copy.18
  27.9 0.0 all-gather.5.cloned.1.call-update
  27.9 1.7 copy.30
  29.5 4.1 all-to-all-start
  33.6 0.0 reduce-scatter.2.cloned.1.call-start
  33.6 1.3 dynamic-slice
  35.5 0.9 dynamic-update-slice
  36.4 344.6 %all-reduce = s32[12288]{0:T(1024)S(1)} all-reduce(s32[12288]{0:T(1024)S(1)} %dynamic-update-slice), channel_id=1, replica_groups=mesh['head'=4,'inner'=4,'outer'=16] {'inner','outer'}, use_global_device_ids=true, to_apply=%add | all-reduce | flops 12288 | bytes 98304
  381.0 2.6 fusion.6
  383.6 0.0 all-to-all-done
  383.6 0.0 all-gather.3.cloned.1.call-done
  383.7 17.7 %fusion = (f32[4,192]{1,0:T(4,128)S(1)}, f32[4,192,12288]{2,1,0:T(8,128)}) fusion(pred[192,12288]{1,0:T(8,128)(4,1)S(1)} %fusion.6, bf16[192,4,128]{2,0,1:T(8,128)(2,1)S(1)} %bitcast.41, bf16[12288,4,128]{2,0,1:T(8,128)(2,1)} %all-gather.3.cloned.1.call-done), kind=kOutput, calls=%fused_computation.2 | convolution fusion | flops 2444229888 | bytes 52890624 | tf_op jit(solution)/shard_map/qhd,khd->hqk/dot_general | solution.py:12
  401.4 17.3 %fusion.1 = f32[4,192]{1,0:T(4,128)S(1)} fusion(f32[4,192,12288]{2,1,0:T(8,128)} %get-tuple-element.6, f32[4,192]{1,0:T(4,128)S(1)} %broadcast_maximum_fusion, pred[192,12288]{1,0:T(8,128)(4,1)S(1)} %fusion.6), kind=kLoop, calls=%fused_computation.3 | loop fusion | flops 37747968 | bytes 40114176 | tf_op jit(solution)/shard_map/reduce_sum | solution.py:17
  418.7 0.0 all-gather.5.cloned.1.call-done
  418.7 20.0 %fusion.16 = bf16[4,24,8,128]{3,2,1,0:T(8,128)(2,1)S(1)} fusion(bf16[12288,4,128]{2,0,1:T(8,128)(2,1)} %all-gather.5.cloned.1.call-done, f32[4,192,12288]{2,1,0:T(8,128)} %get-tuple-element.6, f32[4,192]{1,0:T(4,128)S(1)} %broadcast_maximum_fusion, pred[192,12288]{1,0:T(8,128)(4,1)S(1)} %fusion.6, f32[192,4]{0,1:T(4,128)S(1)} %bitcast.49), kind=kOutput, calls=%fused_computation.13 | convolution fusion | flops 2453864448 | bytes 52893696 | tf_op jit(solution)/shard_map/hqk,khd->hqd/dot_general | solution.py:18
  438.7 4.3 convolution_convert_fusion
  443.0 0.0 reduce-scatter.2.cloned.1.call-update
  443.1 76.2 %reduce-scatter.2.cloned.1.call-done = bf16[48,4096]{1,0:T(8,128)(2,1)} async-done(((bf16[192,4096]{1,0:T(8,128)(2,1)}), bf16[48,4096]{1,0:T(8,128)(2,1)}) %reduce-scatter.2.cloned.1.call-update) | async-done | bytes 393232 | tf_op jit(solution)/shard_map/reduce_scatter | solution.py:83
  (4 shorter events, 0.0 us)
Async XLA Ops:
  6.5 377.1 %all-gather.3.cloned.1.call-start = ((), (), s32[]{:S(2)}) async-start(), calls=%async_computation.4 | async-start | bytes 12779520 | tf_op jit(solution)/shard_map/all_gather | solution.py:73
  18.4 400.3 %all-gather.5.cloned.1.call-start = ((), (), s32[]{:S(2)}) async-start(), calls=%async_computation.5 | async-start | bytes 12779520 | tf_op jit(solution)/shard_map/all_gather | solution.py:74
  29.5 354.1 %all-to-all-start = ((bf16[48,16,128]{2,0,1:T(8,128)(2,1)}), bf16[48,16,128]{2,0,1:T(8,128)(2,1)S(1)}, u32[]{:S(2)}, u32[]{:S(2)}) async-start(bf16[48,16,128]{2,0,1:T(8,128)(2,1)} %bitcast.40), calls=%async_computation | async-start | bytes 393216 | tf_op jit(solution)/shard_map/all_to_all | solution.py:40
  33.6 485.7 %reduce-scatter.2.cloned.1.call-start = ((), (), s32[]{:S(2)}) async-start(), calls=%async_computation.6 | async-start | bytes 1966080 | tf_op jit(solution)/shard_map/reduce_scatter | solution.py:83
Sparse Core Ops, SparseCore 0:
  18.5 142.5 all-gather.2
  164.3 132.9 all-gather.4
  443.2 76.0 reduce-scatter.1
where the time goes:
time: 526 us
  blocking collectives  362 us (69%)
  waiting for transfers between devices  76.3 us (15%)
  matrix products  42 us (8%)
  other arithmetic  19.9 us (4%)
  between operations  13.8 us (3%)
  local copies, waits for them, and re-layouts  7.18 us (1%)
    unnamed x1, blocking collectives  345 us
    reduce_scatter x1, waiting for transfers between devices, body(): lax.psum_scatter(jnp.dot(attended, out_weight, preferred_element_type=jnp...  76.2 us
    dot_general x1, matrix products, online_update(): jnp.einsum('hqk,khd->hqd', weights.astype(jnp.bfloat16), value_block, pre...  20 us
    dot_general x1, matrix products, online_update(): jnp.einsum('qhd,khd->hqk', queries, key_block, preferred_element_type=jnp...  17.7 us
    reduce_sum x1, other arithmetic, online_update(): new_sum = jnp.sum(weights, axis=-1)  17.3 us
  transfers between devices with their start and end apart: 4, of which 1 were waited for; matrix products, arithmetic and copies ran while one was open for 8% of the time, Pallas kernels for 0%

commit v1 on v0

v1 whole, which is shorter than its diff:
```python
import functools
import itertools
import math

import jax
import jax.numpy as jnp
from jax import lax
from jax.experimental import pallas as pl
from jax.experimental.pallas import tpu as pltpu
from jax.sharding import Mesh
from jax.sharding import PartitionSpec as P

SIZES = {"zl": 2, "core": 2, "zh": 4, "y": 4, "x": 4}
AXES = tuple(SIZES)
BLOCK = 192
PART = 96
HALF = 48
HD = 128
EXTRA = 16
OFFSETS = (0, -1, 1, 2)
LOW = -1e30
MASKED = -2e30
RATE = math.log2(math.e) / math.sqrt(HD)


def permute(array, axes, move):
    axes = [a for a in AXES if a in axes]

    def index(at):
        return functools.reduce(lambda n, a: n * SIZES[a] + at[a] % SIZES[a], axes, 0)

    pairs = []
    for spot in itertools.product(*[range(SIZES[a]) for a in axes]):
        at = dict(zip(axes, spot))
        pairs.append((index(at), index({**at, **move(at)})))
    return lax.ppermute(array, tuple(axes), pairs)


def ring(array, first, step):
    second = "y" if first == "x" else "x"

    def move(at):
        axis = first if at["core"] == 0 else second
        return {axis: at[axis] + step}

    return permute(array, ("core", "y", "x"), move)


def attention_kernel(plan, *refs):
    q_refs, kv_refs = refs[0:4], refs[4:8]
    out_refs = refs[8:12]
    q_all, k_all, v_all, top, total, acc = refs[12:]
    swap = plan[0]

    def place(row):
        odd = lax.rem(row // HALF, 2)
        return row + swap * HALF * (1 - 2 * odd)

    for s in range(4):
        for z in range(8):
            i, at = z // 2, (z % 2) * PART
            q_all[i, s * BLOCK + at : s * BLOCK + at + PART, :] = q_refs[s][z, 0:PART, :]
            k_all[4 * s + i, at : at + PART, :] = kv_refs[s][z, EXTRA : EXTRA + PART, :]
            v_all[4 * s + i, at : at + PART, :] = kv_refs[s][z, EXTRA + PART :, :]

    lane = lax.broadcasted_iota(jnp.int32, (1, 4 * BLOCK), 1)
    lane_slot = lane // BLOCK
    lane_place = place(lane - lane_slot * BLOCK)
    row_place = place(lax.broadcasted_iota(jnp.int32, (BLOCK, 1), 0))

    for i in range(4):
        top[...] = jnp.full_like(top, LOW)
        total[...] = jnp.zeros_like(total)
        acc[...] = jnp.zeros_like(acc)
        queries = q_all.at[i]

        def update(kb, masked):
            scores = lax.dot_general(
                k_all[kb], queries[...], (((1,), (1,)), ((), ())), preferred_element_type=jnp.float32
            )
            if masked:
                q_doc = jnp.zeros_like(lane)
                q_base = jnp.zeros_like(lane)
                for s in range(4):
                    doc = jnp.zeros_like(lane)
                    for d in range(1, 8):
                        doc += (plan[80 + 32 * s + 8 * i + d] <= lane_place).astype(jnp.int32)
                    q_doc = jnp.where(lane_slot == s, doc, q_doc)
                    q_base = jnp.where(lane_slot == s, plan[1 + s] + 16 * i, q_base)
                k_doc = jnp.zeros_like(row_place)
                for d in range(1, 8):
                    k_doc += (plan[208 + 8 * kb + d] <= row_place).astype(jnp.int32)
                k_base = plan[5 + kb // 4] + 16 * lax.rem(kb, 4)
                q_pos = q_base * BLOCK + lane_place
                k_pos = k_base * BLOCK + row_place
                scores = jnp.where((k_doc == q_doc) & (k_pos <= q_pos), scores, MASKED)
            old = top[...]
            new = jnp.maximum(old, jnp.max(scores, axis=0, keepdims=True))
            weights = jnp.exp2((scores - new) * RATE)
            keep = jnp.exp2((old - new) * RATE)
            top[...] = new
            total[...] = total[...] * keep + jnp.sum(weights, axis=0, keepdims=True)
            acc[...] = acc[...] * keep + lax.dot_general(
                v_all[kb], weights.astype(jnp.bfloat16), (((0,), (0,)), ((), ())), preferred_element_type=jnp.float32
            )

        def visit(n, carry):
            kb = (n // (i + 1)) * 4 + lax.rem(n, i + 1)
            code = plan[16 + 16 * i + kb]

            @pl.when(code == 1)
            def _():
                update(kb, False)

            @pl.when(code == 2)
            def _():
                update(kb, True)

            return carry

        lax.fori_loop(0, 4 * (i + 1), visit, 0)
        some = total[...] > 0
        scale = jnp.where(some, 1.0 / jnp.where(some, total[...], 1.0), 0.0)
        level = jnp.where(some, top[...] * RATE + jnp.log2(jnp.where(some, total[...], 1.0)), LOW)
        result = (acc[...] * scale).astype(jnp.bfloat16)
        high = level.astype(jnp.bfloat16)
        rest = level - high.astype(jnp.float32)
        middle = rest.astype(jnp.bfloat16)
        low = (rest - middle.astype(jnp.float32)).astype(jnp.bfloat16)
        digits = jnp.concatenate(
            [jnp.broadcast_to(part, (8, 4 * BLOCK)) for part in (high, middle, low, low)], axis=0
        )
        for s in range(4):
            lanes, to = slice(s * BLOCK, (s + 1) * BLOCK), slice(i * BLOCK, (i + 1) * BLOCK)
            out_refs[s][0:HD, to] = result[:, lanes]
            out_refs[s][HD:, to] = digits[:, lanes]


def combine_kernel(where, *refs):
    parts, out_ref, held = refs[0:4], refs[4], refs[5]
    levels = []
    for part in parts:
        digits = part[HD:, :].astype(jnp.float32)
        levels.append(digits[0:1] + digits[8:9] + digits[16:17])
    peak = functools.reduce(jnp.maximum, levels)
    shares = [jnp.exp2(level - peak) for level in levels]
    whole = functools.reduce(jnp.add, shares)
    summed = jnp.zeros((HD, 4 * BLOCK), jnp.float32)
    for part, share in zip(parts, shares):
        summed += part[0:HD, :].astype(jnp.float32) * (share / whole)
    held[...] = summed.T.astype(jnp.bfloat16)
    zl, core = where[0], where[1]
    side = 1 - 2 * core
    for zh in range(4):
        z = 2 * zh + zl
        keep = lax.rem(z + side + 8, 8)
        give = lax.rem(z - side + 8, 8)
        for n, row in enumerate((z * PART, keep * PART, z * PART + HALF, give * PART + HALF)):
            row = pl.multiple_of(row, EXTRA)
            out_ref[zh, n * HALF : (n + 1) * HALF, :] = held[pl.ds(row, HALF), :]


def vmem(n):
    return [pl.BlockSpec(memory_space=pltpu.VMEM)] * n


def attend(plan, queries, keys_values):
    piece = jax.ShapeDtypeStruct((HD + 32, 4 * BLOCK), jnp.bfloat16)
    return pl.pallas_call(
        attention_kernel,
        out_shape=[piece] * 4,
        in_specs=[pl.BlockSpec(memory_space=pltpu.SMEM)] + vmem(8),
        out_specs=vmem(4),
        scratch_shapes=[
            pltpu.VMEM((4, 4 * BLOCK, HD), jnp.bfloat16),
            pltpu.VMEM((16, BLOCK, HD), jnp.bfloat16),
            pltpu.VMEM((16, BLOCK, HD), jnp.bfloat16),
            pltpu.VMEM((1, 4 * BLOCK), jnp.float32),
            pltpu.VMEM((1, 4 * BLOCK), jnp.float32),
            pltpu.VMEM((HD, 4 * BLOCK), jnp.float32),
        ],
        compiler_params=pltpu.CompilerParams(vmem_limit_bytes=40 * 1024 * 1024),
    )(plan, *queries, *keys_values)


def combine(where, pieces):
    return pl.pallas_call(
        combine_kernel,
        out_shape=jax.ShapeDtypeStruct((4, BLOCK, HD), jnp.bfloat16),
        in_specs=[pl.BlockSpec(memory_space=pltpu.SMEM)] + vmem(4),
        out_specs=vmem(1)[0],
        scratch_shapes=[pltpu.VMEM((4 * BLOCK, HD), jnp.bfloat16)],
        compiler_params=pltpu.CompilerParams(vmem_limit_bytes=40 * 1024 * 1024),
    )(where, *pieces)


def make_plan(core, y, x, queries, keys_values):
    def counts(arrays, row):
        return jnp.stack([a[::2, row, :8] for a in arrays]).astype(jnp.int32)

    offsets = jnp.array(OFFSETS, jnp.int32)
    along_x = 4 * y + (x + offsets) % 4
    along_y = 4 * ((y + offsets) % 4) + x
    q_base = jnp.where(core == 0, along_x, along_y)
    k_base = jnp.where(core == 0, along_y, along_x)
    q_counts, k_counts = counts(queries, PART), counts(keys_values, 0)

    def first(c):
        return jnp.sum((c[..., 1:] == 0).astype(jnp.int32), axis=-1)

    def last(c):
        return jnp.sum((c[..., 1:] < BLOCK).astype(jnp.int32), axis=-1)

    step = 16 * jnp.arange(4, dtype=jnp.int32)
    q_at = (q_base[:, None] + step)[:, :, None, None]
    k_at = (k_base[:, None] + step)[None, None]
    q_first, q_last = first(q_counts)[:, :, None, None], last(q_counts)[:, :, None, None]
    k_first, k_last = first(k_counts)[None, None], last(k_counts)[None, None]
    some = jnp.any((q_at >= k_at) & (k_last >= q_first), axis=0)
    full = jnp.all((q_at > k_at) & (k_first == q_last), axis=0)
    code = jnp.where(full, 1, jnp.where(some, 2, 0)).astype(jnp.int32)
    head = jnp.concatenate([core[None], q_base, k_base, jnp.zeros((7,), jnp.int32)])
    return jnp.concatenate([head, code.reshape(-1), q_counts.reshape(-1), k_counts.reshape(-1)])


def body(query, key_in, value, doc_ids, out_weight):
    zl, core, zh, y, x = [lax.axis_index(a).astype(jnp.int32) for a in AXES]

    def heads_of(array, c):
        array = array.reshape(HALF, 2, 2, 4, HD)
        array = lax.dynamic_index_in_dim(array, c, 2, keepdims=False)
        return array.transpose(2, 1, 0, 3).reshape(8, HALF, HD)

    mine = [heads_of(a, core) for a in (query, key_in, value)]
    theirs = jnp.stack([heads_of(a, 1 - core) for a in (query, key_in, value)], axis=1)
    theirs = permute(theirs, ("core",), lambda at: {"core": at["core"] + 1})
    marks = jnp.arange(8, dtype=jnp.int32)
    counts = jnp.sum((doc_ids[None, :] < marks[:, None]).astype(jnp.float32), axis=1).astype(jnp.bfloat16)
    extra = jnp.broadcast_to(jnp.pad(counts, (0, HD - 8)), (8, EXTRA, HD))
    sent = jnp.concatenate(
        [mine[0], theirs[:, 0], extra, mine[1], theirs[:, 1], mine[2], theirs[:, 2]], axis=1
    )
    held = lax.all_to_all(sent, ("zh", "zl"), 0, 0, tiled=True)
    own_q, own_kv = held[:, : PART + EXTRA], held[:, PART:]
    queries = [own_q] + [ring(own_q, "x", -step) for step in OFFSETS[1:]]
    keys_values = [own_kv] + [ring(own_kv, "y", -step) for step in OFFSETS[1:]]
    plan = make_plan(core, y, x, queries, keys_values)
    pieces = attend(plan, queries, keys_values)
    pieces = [pieces[0]] + [ring(p, "x", step) for p, step in zip(pieces[1:], OFFSETS[1:])]
    attended = combine(jnp.stack([zl, core]), pieces)
    attended = lax.all_to_all(attended, "zh", 0, 0, tiled=True)
    attended = attended.transpose(1, 0, 2).reshape(BLOCK, 4 * HD)
    mixed = jnp.dot(attended, out_weight, preferred_element_type=jnp.float32).astype(jnp.bfloat16)
    other = permute(mixed[PART:], ("core",), lambda at: {"core": at["core"] + 1})
    chip = mixed[:PART].astype(jnp.float32) + other.astype(jnp.float32)

    def next_chip(at):
        z = (2 * at["zh"] + at["zl"] + (1 if at["core"] == 0 else -1)) % 8
        return {"zh": z // 2, "zl": z % 2}

    beside = permute(chip[HALF:].astype(jnp.bfloat16), ("zl", "core", "zh"), next_chip)
    return (chip[:HALF] + beside.astype(jnp.float32)).astype(jnp.bfloat16)[None]


def solution(mesh):
    apart = Mesh(mesh.devices.reshape(tuple(SIZES.values())), AXES)
    block, head = ("zh", "y", "x"), ("zl", "core")
    array = P(block, head, None, None)
    return jax.shard_map(
        body,
        mesh=apart,
        in_specs=(array, array, array, P(block), P(head, None)),
        out_specs=P(block, head, None),
        check_vma=False,
    )
```

time: 526 us -> 113 us (0.21)
  the two profiles are of different devices: /device:TPU:1 before, /device:TPU:6 now
where the time goes in v1:
time: 113 us; the launch traced here: 114 us
  waiting for transfers between devices  46.8 us (41%)
  starting transfers between devices  30 us (27%)
  Pallas kernels  12.8 us (11%)
  blocking collectives  11.6 us (10%)
  local copies, waits for them, and re-layouts  7.53 us (7%)
  matrix products  3.23 us (3%)
  other arithmetic  2.06 us (2%)
    ppermute x12, waiting for transfers between devices, permute(): return lax.ppermute(array, tuple(axes), pairs)  26.9 us
    ppermute x12, starting transfers between devices, permute(): return lax.ppermute(array, tuple(axes), pairs)  21.5 us
    all_to_all x1, waiting for transfers between devices, body(): held = lax.all_to_all(sent, ('zh', 'zl'), 0, 0, tiled=True)  19.9 us
    pallas_call x1, Pallas kernels, attend(): pl.pallas_call(attention_kernel, out_shape=[piece] * 4, in_specs=[pl.Bloc...  11.9 us
    all_to_all x1, blocking collectives, body(): attended = lax.all_to_all(attended, 'zh', 0, 0, tiled=True)  11.6 us
    all_to_all x1, starting transfers between devices, body(): held = lax.all_to_all(sent, ('zh', 'zl'), 0, 0, tiled=True)  8.47 us
    unnamed x18, local copies, waits for them, and re-layouts  4.03 us
    dot_general x1, matrix products, body(): jnp.dot(attended, out_weight, preferred_element_type=jnp.float32)  3.23 us
  transfers between devices with their start and end apart: 13, of which 9 were waited for; matrix products, arithmetic and copies ran while one was open for 1% of the time, Pallas kernels for 0%

profile of v1, /device:TPU:6, one launch (start us, length us, event | category | flops | bytes accessed | tf_op | source)
XLA Modules:
  0.0 114.4 jit_solution(8671274716399910389)
XLA Ops:
  0.0 1.0 constant_dynamic-slice_fusion.4
  1.1 1.2 %constant_dynamic-slice_fusion = (bf16[48,2,1,4,128]{4,3,2,1,0:T(4,128)(2,1)S(1)}, bf16[48,2,1,4,128]{4,3,2,1,0:T(4,128)(2,1)S(1)}, bf16[48,2,1,4,128]{4,3,2,1,0:T(4,128)(2,1)S(1)}, bf16[48,2,1,4,128]{4,3,2,1,0:T(4,128)(2,1)S(1)}) fusion(bf16[48,2,2,4,128]{4,3,2,1,0:T(4,128)(2,1)} %bitcast.89, s32[]{:T(128)S(6)} %select_n.53, s32[]{:T(128)S(6)} %select_n.54, ...), kind=kLoop, calls=%fused_computation.40 | loop fusion | bytes 786440 | tf_op jit(solution)/shard_map/jit(dynamic_index_in_dim)/dynamic_slice | solution.py:231
  2.3 0.1 collective-permute-start
  2.5 0.0 copy-start
  2.5 0.1 convert_reduce_fusion.4
  2.6 0.7 constant_dynamic-update-slice_fusion.3
  3.3 0.7 collective-permute-done
  4.0 0.7 fusion.6
  4.7 0.6 constant_dynamic-update-slice_fusion.2
  5.3 0.7 constant_dynamic-update-slice_fusion.1
  6.0 0.7 fusion.5
  6.6 0.7 constant_dynamic-update-slice_fusion
  7.3 0.7 fusion.4
  8.0 8.5 %all-to-all-start = ((bf16[8,304,128]{2,1,0:T(8,128)(2,1)}), bf16[8,304,128]{2,1,0:T(8,128)(2,1)S(1)}, u32[]{:S(2)}, u32[]{:S(2)}) async-start(bf16[8,304,128]{2,1,0:T(8,128)(2,1)} %fusion.4), calls=%async_computation | async-start | bytes 1245184 | tf_op jit(solution)/shard_map/all_to_all | solution.py:243
  16.4 19.9 %all-to-all-done = bf16[8,304,128]{2,1,0:T(8,128)(2,1)S(1)} async-done(((bf16[8,304,128]{2,1,0:T(8,128)(2,1)}), bf16[8,304,128]{2,1,0:T(8,128)(2,1)S(1)}, u32[]{:S(2)}, u32[]{:S(2)}) %all-to-all-start) | async-done | bytes 622624 | tf_op jit(solution)/shard_map/all_to_all | solution.py:243
  36.4 1.5 %collective-permute-start.6 = (bf16[8,112,128]{2,1,0:T(8,128)(2,1)S(1)}, bf16[8,112,128]{2,1,0:T(8,128)(2,1)S(1)}, u32[]{:S(2)}, u32[]{:S(2)}) collective-permute-start(bf16[8,112,128]{2,1,0:T(8,128)(2,1)S(1)} %slice.92.refs_0_), channel_id=1, source_target_pairs={{0,2},{1,3},{2,0},{3,1},{4,6},{5,7},{6,4},{7,5},{8,10},{9,11},{10,... | collective-permute-start | bytes 688136 | tf_op jit(solution)/shard_map/ppermute | solution.py:36
  37.9 0.1 collective-permute-start.5
  38.0 3.2 %collective-permute-start.4 = (bf16[8,112,128]{2,1,0:T(8,128)(2,1)S(1)}, bf16[8,112,128]{2,1,0:T(8,128)(2,1)S(1)}, u32[]{:S(2)}, u32[]{:S(2)}) collective-permute-start(bf16[8,112,128]{2,1,0:T(8,128)(2,1)S(1)} %slice.92.refs_0_), channel_id=1, source_target_pairs={{0,1},{1,2},{2,3},{3,0},{4,5},{5,6},{6,7},{7,4},{8,9},{9,10},{10,1... | collective-permute-start | bytes 688136 | tf_op jit(solution)/shard_map/ppermute | solution.py:36
  41.2 3.3 %collective-permute-start.3 = (bf16[8,208,128]{2,1,0:T(8,128)(2,1)S(1)}, bf16[8,208,128]{2,1,0:T(8,128)(2,1)S(1)}, u32[]{:S(2)}, u32[]{:S(2)}) collective-permute-start(bf16[8,208,128]{2,1,0:T(8,128)(2,1)S(1)} %slice.90.refs_4_), channel_id=1, source_target_pairs={{0,8},{1,9},{2,10},{3,11},{4,12},{5,13},{6,14},{7,15},{8,0},{9,1},... | collective-permute-start | bytes 1277960 | tf_op jit(solution)/shard_map/ppermute | solution.py:36
  44.5 1.1 collective-permute-start.2
  45.6 1.0 collective-permute-start.1
  46.5 0.1 broadcast_add_fusion.1
  46.7 5.1 %collective-permute-done.5.refs_2_ = bf16[8,112,128]{2,1,0:T(8,128)(2,1)S(1)} collective-permute-done((bf16[8,112,128]{2,1,0:T(8,128)(2,1)S(1)}, bf16[8,112,128]{2,1,0:T(8,128)(2,1)S(1)}, u32[]{:S(2)}, u32[]{:S(2)}) %collective-permute-start.5) | collective-permute-done | bytes 229408 | tf_op jit(solution)/shard_map/ppermute | solution.py:36
  51.8 0.1 reshape.110
  51.9 0.3 convert_reduce_fusion
  52.2 3.7 %collective-permute-done.2.refs_6_ = bf16[8,208,128]{2,1,0:T(8,128)(2,1)S(1)} collective-permute-done((bf16[8,208,128]{2,1,0:T(8,128)(2,1)S(1)}, bf16[8,208,128]{2,1,0:T(8,128)(2,1)S(1)}, u32[]{:S(2)}, u32[]{:S(2)}) %collective-permute-start.2) | collective-permute-done | bytes 426016 | tf_op jit(solution)/shard_map/ppermute | solution.py:36
  55.9 0.1 reshape.111
  56.0 0.3 convert_reduce_fusion.1
  56.3 0.1 and_reduce_fusion
  56.5 0.1 select_n.57
  56.6 0.1 concatenate.7.plan
  56.7 11.9 %shard_map.64 = (bf16[160,768]{1,0:T(8,128)(2,1)S(1)}, bf16[160,768]{1,0:T(8,128)(2,1)}, bf16[160,768]{1,0:T(8,128)(2,1)S(1)}, bf16[160,768]{1,0:T(8,128)(2,1)S(1)}) custom-call(s32[336]{0:T(512)S(1)} %concatenate.7.plan, bf16[8,112,128]{2,1,0:T(8,128)(2,1)S(1)} %slice.92.refs_0_, bf16[8,112,128]{2,1,0:T(8,128)(2,1)S(1)} %collective-permute-done.4.refs_1_, ...), custom_call_target="tpu_custom_call" | custom-call | tf_op jit(solution)/shard_map/pallas_call | solution.py:169
  68.6 3.2 %collective-permute-start.8 = (bf16[160,768]{1,0:T(8,128)(2,1)S(1)}, bf16[160,768]{1,0:T(8,128)(2,1)S(1)}, u32[]{:S(2)}, u32[]{:S(2)}) collective-permute-start(bf16[160,768]{1,0:T(8,128)(2,1)S(1)} %get-tuple-element.11), channel_id=1, source_target_pairs={{0,1},{1,2},{2,3},{3,0},{4,5},{5,6},{6,7},{7,4},{8,9},{9,10},{10,1... | collective-permute-start | bytes 737288 | tf_op jit(solution)/shard_map/ppermute | solution.py:36
  71.9 0.0 collective-permute-start.9
  71.9 0.1 pad_add_fusion.where
  71.9 4.3 %collective-permute-done.7.refs_1_ = bf16[160,768]{1,0:T(8,128)(2,1)S(1)} collective-permute-done((bf16[160,768]{1,0:T(8,128)(2,1)}, bf16[160,768]{1,0:T(8,128)(2,1)S(1)}, u32[]{:S(2)}, u32[]{:S(2)}) %collective-permute-start.7) | collective-permute-done | bytes 245792 | tf_op jit(solution)/shard_map/ppermute | solution.py:36
  76.2 2.0 %collective-permute-done.8.refs_2_ = bf16[160,768]{1,0:T(8,128)(2,1)S(1)} collective-permute-done((bf16[160,768]{1,0:T(8,128)(2,1)S(1)}, bf16[160,768]{1,0:T(8,128)(2,1)S(1)}, u32[]{:S(2)}, u32[]{:S(2)}) %collective-permute-start.8) | collective-permute-done | bytes 245792 | tf_op jit(solution)/shard_map/ppermute | solution.py:36
  78.2 1.4 %collective-permute-done.9.refs_3_ = bf16[160,768]{1,0:T(8,128)(2,1)S(1)} collective-permute-done((bf16[160,768]{1,0:T(8,128)(2,1)S(1)}, bf16[160,768]{1,0:T(8,128)(2,1)S(1)}, u32[]{:S(2)}, u32[]{:S(2)}) %collective-permute-start.9) | collective-permute-done | bytes 245792 | tf_op jit(solution)/shard_map/ppermute | solution.py:36
  79.6 0.8 shard_map.65
  80.4 11.6 %all_to_all.10 = bf16[4,192,128]{2,1,0:T(8,128)(2,1)S(1)} all-to-all(bf16[4,192,128]{2,1,0:T(8,128)(2,1)S(1)} %shard_map.65), channel_id=1, replica_groups=mesh['zl'=2,'core'=2,'zh'=4,'y'=4,'x'=4] {'zh'}, dimensions={0} | all-to-all | bytes 393216 | tf_op jit(solution)/shard_map/all_to_all | solution.py:251
  92.0 3.2 %convolution_convert_fusion = bf16[192,4096]{1,0:T(8,128)(2,1)S(1)} fusion(bf16[512,4096]{1,0:T(8,128)(2,1)} %param.10, bf16[4,192,128]{2,1,0:T(8,128)(2,1)S(1)} %all_to_all.10), kind=kOutput, calls=%fused_computation | convolution fusion | flops 806092800 | bytes 5963776 | tf_op jit(solution)/shard_map/dot_general | solution.py:253
  95.2 0.1 slice.95
  95.3 7.0 %collective-permute-start.10 = (bf16[96,4096]{1,0:T(8,128)(2,1)S(1)}, bf16[96,4096]{1,0:T(8,128)(2,1)S(1)}, u32[]{:S(2)}, u32[]{:S(2)}) collective-permute-start(bf16[96,4096]{1,0:T(8,128)(2,1)S(1)} %slice.95), channel_id=1, source_target_pairs={{0,64},{64,0},{1,65},{65,1},{2,66},{66,2},{3,67},{67,3},{4,68},{68... | collective-permute-start | bytes 2359304 | tf_op jit(solution)/shard_map/ppermute | solution.py:36
  102.3 1.9 %collective-permute-done.10 = bf16[96,4096]{1,0:T(8,128)(2,1)S(1)} collective-permute-done((bf16[96,4096]{1,0:T(8,128)(2,1)S(1)}, bf16[96,4096]{1,0:T(8,128)(2,1)S(1)}, u32[]{:S(2)}, u32[]{:S(2)}) %collective-permute-start.10) | collective-permute-done | bytes 786464 | tf_op jit(solution)/shard_map/ppermute | solution.py:36
  104.2 0.2 convert_add_fusion
  104.5 1.1 collective-permute-start.11
  105.6 8.0 %collective-permute-done.11 = bf16[48,4096]{1,0:T(8,128)(2,1)S(1)} collective-permute-done((bf16[48,4096]{1,0:T(8,128)(2,1)S(1)}, bf16[48,4096]{1,0:T(8,128)(2,1)S(1)}, u32[]{:S(2)}, u32[]{:S(2)}) %collective-permute-start.11) | collective-permute-done | bytes 393248 | tf_op jit(solution)/shard_map/ppermute | solution.py:36
  113.5 0.8 fusion.1
  (41 shorter events, 0.4 us)
Async XLA Ops:
  0.0 2.5 %copy-start.1 = (s32[192]{0:T(256)S(1)}, s32[192]{0:T(256)}, u32[]{:S(2)}) copy-start(s32[192]{0:T(256)} %param.9) | copy-start | bytes 2308
  2.3 1.7 %collective-permute-start = (bf16[8,3,48,128]{3,2,0,1:T(8,128)(2,1)S(1)}, bf16[8,3,48,128]{3,2,0,1:T(8,128)(2,1)S(1)}, u32[]{:S(2)}, u32[]{:S(2)}) collective-permute-start(bf16[8,3,48,128]{3,2,0,1:T(8,128)(2,1)S(1)} %pad_maximum_fusion), channel_id=1, source_target_pairs={{0,64},{64,0},{1,65},{65,1},{2,66},{66,2},{3,67},{67,3},{4,68},{68... | collective-permute-start | bytes 884744 | tf_op jit(solution)/shard_map/ppermute | solution.py:36
  2.5 35.4 %copy-start = (s32[4]{0:T(128)S(1)}, s32[4]{0:T(128)}, u32[]{:S(2)}) copy-start(s32[4]{0:T(128)} %constant.74.clone) | copy-start | bytes 52
  8.0 28.4 %all-to-all-start = ((bf16[8,304,128]{2,1,0:T(8,128)(2,1)}), bf16[8,304,128]{2,1,0:T(8,128)(2,1)S(1)}, u32[]{:S(2)}, u32[]{:S(2)}) async-start(bf16[8,304,128]{2,1,0:T(8,128)(2,1)} %fusion.4), calls=%async_computation | async-start | bytes 1245184 | tf_op jit(solution)/shard_map/all_to_all | solution.py:243
  36.4 9.2 %collective-permute-start.6 = (bf16[8,112,128]{2,1,0:T(8,128)(2,1)S(1)}, bf16[8,112,128]{2,1,0:T(8,128)(2,1)S(1)}, u32[]{:S(2)}, u32[]{:S(2)}) collective-permute-start(bf16[8,112,128]{2,1,0:T(8,128)(2,1)S(1)} %slice.92.refs_0_), channel_id=1, source_target_pairs={{0,2},{1,3},{2,0},{3,1},{4,6},{5,7},{6,4},{7,5},{8,10},{9,11},{10,... | collective-permute-start | bytes 688136 | tf_op jit(solution)/shard_map/ppermute | solution.py:36
  37.9 13.9 %collective-permute-start.5 = (bf16[8,112,128]{2,1,0:T(8,128)(2,1)S(1)}, bf16[8,112,128]{2,1,0:T(8,128)(2,1)S(1)}, u32[]{:S(2)}, u32[]{:S(2)}) collective-permute-start(bf16[8,112,128]{2,1,0:T(8,128)(2,1)S(1)} %slice.92.refs_0_), channel_id=1, source_target_pairs={{0,3},{1,0},{2,1},{3,2},{4,7},{5,4},{6,5},{7,6},{8,11},{9,8},{10,9... | collective-permute-start | bytes 688136 | tf_op jit(solution)/shard_map/ppermute | solution.py:36
  38.0 13.8 %collective-permute-start.4 = (bf16[8,112,128]{2,1,0:T(8,128)(2,1)S(1)}, bf16[8,112,128]{2,1,0:T(8,128)(2,1)S(1)}, u32[]{:S(2)}, u32[]{:S(2)}) collective-permute-start(bf16[8,112,128]{2,1,0:T(8,128)(2,1)S(1)} %slice.92.refs_0_), channel_id=1, source_target_pairs={{0,1},{1,2},{2,3},{3,0},{4,5},{5,6},{6,7},{7,4},{8,9},{9,10},{10,1... | collective-permute-start | bytes 688136 | tf_op jit(solution)/shard_map/ppermute | solution.py:36
  41.2 11.0 %collective-permute-start.3 = (bf16[8,208,128]{2,1,0:T(8,128)(2,1)S(1)}, bf16[8,208,128]{2,1,0:T(8,128)(2,1)S(1)}, u32[]{:S(2)}, u32[]{:S(2)}) collective-permute-start(bf16[8,208,128]{2,1,0:T(8,128)(2,1)S(1)} %slice.90.refs_4_), channel_id=1, source_target_pairs={{0,8},{1,9},{2,10},{3,11},{4,12},{5,13},{6,14},{7,15},{8,0},{9,1},... | collective-permute-start | bytes 1277960 | tf_op jit(solution)/shard_map/ppermute | solution.py:36
  44.5 11.4 %collective-permute-start.2 = (bf16[8,208,128]{2,1,0:T(8,128)(2,1)S(1)}, bf16[8,208,128]{2,1,0:T(8,128)(2,1)S(1)}, u32[]{:S(2)}, u32[]{:S(2)}) collective-permute-start(bf16[8,208,128]{2,1,0:T(8,128)(2,1)S(1)} %slice.90.refs_4_), channel_id=1, source_target_pairs={{0,12},{1,13},{2,14},{3,15},{4,0},{5,1},{6,2},{7,3},{8,4},{9,5},{1... | collective-permute-start | bytes 1277960 | tf_op jit(solution)/shard_map/ppermute | solution.py:36
  45.6 10.3 %collective-permute-start.1 = (bf16[8,208,128]{2,1,0:T(8,128)(2,1)S(1)}, bf16[8,208,128]{2,1,0:T(8,128)(2,1)S(1)}, u32[]{:S(2)}, u32[]{:S(2)}) collective-permute-start(bf16[8,208,128]{2,1,0:T(8,128)(2,1)S(1)} %slice.90.refs_4_), channel_id=1, source_target_pairs={{0,4},{1,5},{2,6},{3,7},{4,8},{5,9},{6,10},{7,11},{8,12},{9,13},{1... | collective-permute-start | bytes 1277960 | tf_op jit(solution)/shard_map/ppermute | solution.py:36
  68.6 7.6 %collective-permute-start.7 = (bf16[160,768]{1,0:T(8,128)(2,1)}, bf16[160,768]{1,0:T(8,128)(2,1)S(1)}, u32[]{:S(2)}, u32[]{:S(2)}) collective-permute-start(bf16[160,768]{1,0:T(8,128)(2,1)} %get-tuple-element.10), channel_id=1, source_target_pairs={{0,3},{1,0},{2,1},{3,2},{4,7},{5,4},{6,5},{7,6},{8,11},{9,8},{10,9... | collective-permute-start | bytes 737288 | tf_op jit(solution)/shard_map/ppermute | solution.py:36
  68.6 9.6 %collective-permute-start.8 = (bf16[160,768]{1,0:T(8,128)(2,1)S(1)}, bf16[160,768]{1,0:T(8,128)(2,1)S(1)}, u32[]{:S(2)}, u32[]{:S(2)}) collective-permute-start(bf16[160,768]{1,0:T(8,128)(2,1)S(1)} %get-tuple-element.11), channel_id=1, source_target_pairs={{0,1},{1,2},{2,3},{3,0},{4,5},{5,6},{6,7},{7,4},{8,9},{9,10},{10,1... | collective-permute-start | bytes 737288 | tf_op jit(solution)/shard_map/ppermute | solution.py:36
  71.9 7.7 %collective-permute-start.9 = (bf16[160,768]{1,0:T(8,128)(2,1)S(1)}, bf16[160,768]{1,0:T(8,128)(2,1)S(1)}, u32[]{:S(2)}, u32[]{:S(2)}) collective-permute-start(bf16[160,768]{1,0:T(8,128)(2,1)S(1)} %get-tuple-element.12), channel_id=1, source_target_pairs={{0,2},{1,3},{2,0},{3,1},{4,6},{5,7},{6,4},{7,5},{8,10},{9,11},{10,... | collective-permute-start | bytes 737288 | tf_op jit(solution)/shard_map/ppermute | solution.py:36
  95.3 8.9 %collective-permute-start.10 = (bf16[96,4096]{1,0:T(8,128)(2,1)S(1)}, bf16[96,4096]{1,0:T(8,128)(2,1)S(1)}, u32[]{:S(2)}, u32[]{:S(2)}) collective-permute-start(bf16[96,4096]{1,0:T(8,128)(2,1)S(1)} %slice.95), channel_id=1, source_target_pairs={{0,64},{64,0},{1,65},{65,1},{2,66},{66,2},{3,67},{67,3},{4,68},{68... | collective-permute-start | bytes 2359304 | tf_op jit(solution)/shard_map/ppermute | solution.py:36
  104.5 9.1 %collective-permute-start.11 = (bf16[48,4096]{1,0:T(8,128)(2,1)S(1)}, bf16[48,4096]{1,0:T(8,128)(2,1)S(1)}, u32[]{:S(2)}, u32[]{:S(2)}) collective-permute-start(bf16[48,4096]{1,0:T(8,128)(2,1)S(1)} %slice.130), channel_id=1, source_target_pairs={{0,128},{16,144},{32,160},{48,176},{64,240},{80,192},{96,208},{112... | collective-permute-start | bytes 1179656 | tf_op jit(solution)/shard_map/ppermute | solution.py:36

commit v2 on v1

v2 whole, which is shorter than its diff:
```python
import functools
import itertools
import math

import jax
import jax.numpy as jnp
from jax import lax
from jax.experimental import pallas as pl
from jax.experimental.pallas import tpu as pltpu
from jax.sharding import Mesh
from jax.sharding import PartitionSpec as P

SIZES = {"zl": 2, "core": 2, "zh": 4, "y": 4, "x": 4}
AXES = tuple(SIZES)
BLOCK = 192
PART = 96
HALF = 48
HD = 128
EXTRA = 16
OFFSETS = (0, 1, 2, -1)
LOW = -1e30
MASKED = -2e30
SPAN = 1 << 14
WIDE = 2 * BLOCK
GROUPS = 8
SPARE = 16
RATE = math.log2(math.e) / math.sqrt(HD)


def permute(array, axes, move):
    axes = [a for a in AXES if a in axes]

    def index(at):
        return functools.reduce(lambda n, a: n * SIZES[a] + at[a] % SIZES[a], axes, 0)

    pairs = []
    for spot in itertools.product(*[range(SIZES[a]) for a in axes]):
        at = dict(zip(axes, spot))
        pairs.append((index(at), index({**at, **move(at)})))
    return lax.ppermute(array, tuple(axes), pairs)


def ring(array, first, step):
    second = "y" if first == "x" else "x"

    def move(at):
        axis = first if at["core"] == 0 else second
        return {axis: at[axis] + step}

    return permute(array, ("core", "y", "x"), move)


def at_spot():
    return [lax.axis_index(a).astype(jnp.int32) for a in AXES]


def attention_kernel(*refs):
    q_refs, kv_refs, out_ref = refs[0:4], refs[4:8], refs[8]
    q_all, k_all, v_all, k_code, q_code, top, total, acc = refs[9:17]
    scores_of, weights_of, keep_of, peak_of = refs[17:19], refs[19:21], refs[21:23], refs[23:25]
    tile_keys, tile_group, table, plan, sent = refs[25:30]
    _, swap, _, y, x = at_spot()
    mine = jnp.where(swap == 0, x, y)
    theirs = jnp.where(swap == 0, y, x)

    def place(row):
        odd = lax.rem(row // HALF, 2)
        return row + swap * HALF * (1 - 2 * odd)

    def slot_of(at):
        return lax.rem(at - mine + 4, 4)

    def q_base(at):
        return jnp.where(swap == 0, 4 * y + at, 4 * at + x)

    def k_base(at):
        return jnp.where(swap == 0, 4 * at + x, 4 * y + at)

    for s in range(4):
        for i in range(4):
            n = 4 * s + i
            q_row = q_refs[s][2 * i, PART : PART + EXTRA, :].astype(jnp.float32)
            k_row = kv_refs[s][2 * i, 0:EXTRA, :].astype(jnp.float32)
            table[n : n + 1, :] = q_row[0:1].astype(jnp.int32)
            table[16 + n : 17 + n, :] = k_row[0:1].astype(jnp.int32)
    counts = table[...]
    row = lax.broadcasted_iota(jnp.int32, counts.shape, 0)
    lane = lax.broadcasted_iota(jnp.int32, counts.shape, 1)

    def tally(mask, axis):
        return jnp.sum(jnp.where(mask, 1.0, 0.0), axis=axis, keepdims=True)

    inner = (lane >= 1) & (lane < 8)
    first, last = tally(inner & (counts == 0), 1), tally(inner & (counts < BLOCK), 1)
    k_last = jnp.sum(jnp.where(row == lane + 16, last, 0.0), axis=0, keepdims=True)
    q_at = q_base(lax.rem(mine + row // 4, 4)) + 16 * lax.rem(row, 4)
    k_at = k_base(lax.rem(theirs + lane // 4, 4)) + 16 * lax.rem(lane, 4)
    some = (q_at >= k_at) & (k_last >= first) & (lane < 16)
    bits = jnp.sum(jnp.where(some, lax.shift_left(1, jnp.minimum(lane, 16)).astype(jnp.float32), 0.0), axis=1, keepdims=True)
    for at, column in ((8, first), (9, last), (10, bits)):
        counts = jnp.where(lane == at, column.astype(jnp.int32), counts)
    table[...] = counts
    copy = pltpu.make_async_copy(table, plan, sent)
    copy.start()

    for s in range(4):
        at = lax.rem(mine + s, 4) * BLOCK
        for z in range(8):
            i, row = z // 2, (z % 2) * PART
            to = pl.multiple_of(at + row, PART)
            q_all[i, pl.ds(to, PART), :] = q_refs[s][z, 0:PART, :]
            k_all[4 * s + i, row : row + PART, :] = kv_refs[s][z, EXTRA : EXTRA + PART, :]
            v_all[4 * s + i, row : row + PART, :] = kv_refs[s][z, EXTRA + PART :, :]
    k_all[SPARE] = jnp.zeros((BLOCK, HD), jnp.bfloat16)
    v_all[SPARE] = jnp.zeros((BLOCK, HD), jnp.bfloat16)
    top[...] = jnp.full_like(top, LOW)
    total[...] = jnp.zeros_like(total)
    acc[...] = jnp.zeros_like(acc)
    copy.wait()

    def clear(n):
        tile_keys[2 * n] = SPARE
        tile_keys[2 * n + 1] = SPARE
        tile_group[n] = GROUPS

    clear(0)
    clear(1)
    end = jnp.int32(4)
    for group in range(GROUPS):
        i, first = group // 2, 2 * (group % 2)
        bits = plan[4 * slot_of(first) + i, 10] | plan[4 * slot_of(first + 1) + i, 10]
        for slot in range(4):
            for j in range(i + 1):
                kb = 4 * slot + j
                tile_keys[end] = kb
                tile_group[end // 2] = group
                end = end + (lax.shift_right_logical(bits, kb) & 1)
        tile_keys[end] = SPARE
        end = ((end + 1) // 2) * 2
    tiles = end // 2
    for n in range(4):
        clear(tiles + n)

    row_place = place(lax.broadcasted_iota(jnp.int32, (BLOCK, HD), 0))
    for kb in range(16):
        base = (k_base(lax.rem(theirs + kb // 4, 4)) + 16 * (kb % 4)) * BLOCK
        first, last = plan[16 + kb, 8], plan[16 + kb, 9]
        k_code[kb] = (row_place + (base + first * SPAN)).astype(jnp.uint32)

        def add(d, carry, kb=kb):
            k_code[kb] += jnp.where(plan[16 + kb, d] <= row_place, SPAN, 0).astype(jnp.uint32)
            return carry

        lax.fori_loop(first + 1, last + 1, add, 0)
    k_code[SPARE] = jnp.full((BLOCK, HD), 1 << 30, jnp.uint32)
    lane = lax.broadcasted_iota(jnp.int32, (1, WIDE), 1)
    second = lane >= BLOCK
    lane_place = place(jnp.where(second, lane - BLOCK, lane))
    for group in range(GROUPS):
        i, first = group // 2, 2 * (group % 2)
        slots = [slot_of(first), slot_of(first + 1)]
        code = lane_place + jnp.where(second, q_base(first + 1), q_base(first)) * BLOCK + 16 * i * BLOCK
        for d in range(1, 8):
            counts = [plan[4 * slot + i, d] for slot in slots]
            code += jnp.where(jnp.where(second, counts[1], counts[0]) <= lane_place, SPAN, 0)
        q_code[group] = code.astype(jnp.uint32)
    q_code[GROUPS] = jnp.zeros((1, WIDE), jnp.uint32)

    def stage(n, odd):
        group = tile_group[n + 2]
        row = pl.multiple_of(lax.rem(group, 2) * WIDE, WIDE)
        queries = q_all[group // 2, pl.ds(row, WIDE), :]
        q_row = q_code[group]
        peaks = []
        for half in range(2):
            kb = tile_keys[2 * n + 4 + half]
            scores = lax.dot_general(
                k_all[kb], queries, (((1,), (1,)), ((), ())), preferred_element_type=jnp.float32
            )
            ahead = q_row - jnp.concatenate([k_code[kb]] * (WIDE // HD), axis=1)
            scores = jnp.where(ahead < SPAN, scores, MASKED)
            scores_of[odd][half * BLOCK : (half + 1) * BLOCK, :] = scores
            peaks.append(jnp.max(scores, axis=0, keepdims=True))
        peak_of[odd][...] = jnp.maximum(peaks[0], peaks[1])

        group = tile_group[n + 1]
        old = top[group]
        new = jnp.maximum(old, peak_of[1 - odd][...])
        keep = jnp.exp2((old - new) * RATE)
        top[group] = new
        keep_of[1 - odd][...] = keep
        weights = jnp.exp2((scores_of[1 - odd][...] - new) * RATE)
        total[group] = total[group] * keep + jnp.sum(weights, axis=0, keepdims=True)
        weights_of[1 - odd][...] = weights.astype(jnp.bfloat16)

        group = tile_group[n]
        product = acc[group] * keep_of[odd][...]
        for half in range(2):
            product += lax.dot_general(
                v_all[tile_keys[2 * n + half]],
                weights_of[odd][half * BLOCK : (half + 1) * BLOCK, :],
                (((0,), (0,)), ((), ())),
                preferred_element_type=jnp.float32,
            )
        acc[group] = product

    def step(n, carry):
        stage(2 * n, 0)
        stage(2 * n + 1, 1)
        return carry

    lax.fori_loop(0, (tiles + 1) // 2, step, 0)

    for group in range(GROUPS):
        i, first = group // 2, 2 * (group % 2)
        some = total[group] > 0
        whole = jnp.where(some, total[group], 1.0)
        level = jnp.where(some, top[group] * RATE + jnp.log2(whole), LOW)
        result = (acc[group] * jnp.where(some, 1.0 / whole, 0.0)).astype(jnp.bfloat16)
        high = level.astype(jnp.bfloat16)
        rest = level - high.astype(jnp.float32)
        middle = rest.astype(jnp.bfloat16)
        low = rest - middle.astype(jnp.float32)
        row = lax.broadcasted_iota(jnp.int32, (EXTRA, WIDE), 0)
        digits = jnp.where(row == 0, high.astype(jnp.float32), jnp.where(row == 1, middle.astype(jnp.float32), low))
        digits = digits.astype(jnp.bfloat16)
        for half in range(2):
            slot = slot_of(first + half)
            lanes, to = slice(half * BLOCK, (half + 1) * BLOCK), slice(i * BLOCK, (i + 1) * BLOCK)
            out_ref[slot, 0:HD, to] = result[:, lanes]
            out_ref[slot, HD:, to] = digits[:, lanes]


def combine_kernel(*refs):
    parts, out_ref = refs[0:4], refs[4]
    levels = []
    for part in parts:
        digits = part[HD:, :].astype(jnp.float32)
        levels.append(digits[0:1] + digits[1:2] + digits[2:3])
    peak = functools.reduce(jnp.maximum, levels)
    shares = [jnp.exp2(level - peak) for level in levels]
    whole = functools.reduce(jnp.add, shares)
    summed = jnp.zeros((HD, 4 * BLOCK), jnp.float32)
    for part, share in zip(parts, shares):
        summed += part[0:HD, :].astype(jnp.float32) * (share / whole)
    out_ref[...] = summed.T.astype(jnp.bfloat16)


def project_kernel(heads_ref, own_ref, beside_ref, out_ref, held):
    zl, tile = at_spot()[0], 1024
    for zh in range(4):
        columns = slice(zh * HD, (zh + 1) * HD)
        held[0, :, columns] = heads_ref[2 * zh + zl]
        held[1, :, columns] = heads_ref[2 * zh + 1 - zl]

    def step(n, carry):
        columns = pl.ds(pl.multiple_of(n * tile, tile), tile)
        product = jnp.dot(held[0], own_ref[:, columns], preferred_element_type=jnp.float32)
        product += jnp.dot(held[1], beside_ref[:, columns], preferred_element_type=jnp.float32)
        out_ref[:, columns] = product.astype(jnp.bfloat16)
        return carry

    lax.fori_loop(0, out_ref.shape[1] // tile, step, 0)


def vmem(n):
    return [pl.BlockSpec(memory_space=pltpu.VMEM)] * n


def attend(queries, keys_values):
    block = (SPARE + 1, BLOCK, HD)
    row = (GROUPS + 1, 1, WIDE)
    return pl.pallas_call(
        attention_kernel,
        out_shape=jax.ShapeDtypeStruct((4, HD + EXTRA, 4 * BLOCK), jnp.bfloat16),
        in_specs=vmem(8),
        out_specs=vmem(1)[0],
        scratch_shapes=[
            pltpu.VMEM((GROUPS // 2 + 1, 4 * BLOCK, HD), jnp.bfloat16),
            pltpu.VMEM(block, jnp.bfloat16),
            pltpu.VMEM(block, jnp.bfloat16),
            pltpu.VMEM(block, jnp.uint32),
            pltpu.VMEM(row, jnp.uint32),
            pltpu.VMEM(row, jnp.float32),
            pltpu.VMEM(row, jnp.float32),
            pltpu.VMEM((GROUPS + 1, HD, WIDE), jnp.float32),
            pltpu.VMEM((WIDE, WIDE), jnp.float32),
            pltpu.VMEM((WIDE, WIDE), jnp.float32),
            pltpu.VMEM((WIDE, WIDE), jnp.bfloat16),
            pltpu.VMEM((WIDE, WIDE), jnp.bfloat16),
            pltpu.VMEM((1, WIDE), jnp.float32),
            pltpu.VMEM((1, WIDE), jnp.float32),
            pltpu.VMEM((1, WIDE), jnp.float32),
            pltpu.VMEM((1, WIDE), jnp.float32),
            pltpu.SMEM((192,), jnp.int32),
            pltpu.SMEM((96,), jnp.int32),
            pltpu.VMEM((32, HD), jnp.int32),
            pltpu.SMEM((32, HD), jnp.int32),
            pltpu.SemaphoreType.DMA,
        ],
        compiler_params=pltpu.CompilerParams(vmem_limit_bytes=10 * 1024 * 1024),
    )(*queries, *keys_values)


def combine(pieces):
    return pl.pallas_call(
        combine_kernel,
        out_shape=jax.ShapeDtypeStruct((4 * BLOCK, HD), jnp.bfloat16),
        in_specs=vmem(4),
        out_specs=vmem(1)[0],
        compiler_params=pltpu.CompilerParams(vmem_limit_bytes=8 * 1024 * 1024),
    )(*pieces)


def project(heads, own, beside):
    return pl.pallas_call(
        project_kernel,
        out_shape=jax.ShapeDtypeStruct((PART, own.shape[1]), jnp.bfloat16),
        in_specs=vmem(3),
        out_specs=vmem(1)[0],
        scratch_shapes=[pltpu.VMEM((2, PART, 4 * HD), jnp.bfloat16)],
        compiler_params=pltpu.CompilerParams(vmem_limit_bytes=10 * 1024 * 1024),
    )(heads, own, beside)


def body(query, key_in, value, doc_ids, out_weight):
    core = lax.axis_index("core").astype(jnp.int32)

    def heads_of(array, c):
        array = array.reshape(HALF, 2, 2, 4, HD)
        array = lax.dynamic_index_in_dim(array, c, 2, keepdims=False)
        return array.transpose(2, 1, 0, 3).reshape(8, HALF, HD)

    mine = [heads_of(a, core) for a in (query, key_in, value)]
    theirs = jnp.stack([heads_of(a, 1 - core) for a in (query, key_in, value)], axis=1)
    theirs = permute(theirs, ("core",), lambda at: {"core": at["core"] + 1})
    marks = jnp.arange(8, dtype=jnp.int32)
    counts = jnp.sum((doc_ids[None, :] < marks[:, None]).astype(jnp.float32), axis=1).astype(jnp.bfloat16)
    extra = jnp.broadcast_to(jnp.pad(counts, (0, HD - 8)), (8, EXTRA, HD))
    sent = jnp.concatenate(
        [mine[0], theirs[:, 0], extra, mine[1], theirs[:, 1], mine[2], theirs[:, 2]], axis=1
    )
    held = lax.all_to_all(sent, ("zh", "zl"), 0, 0, tiled=True)
    held, weight = lax.optimization_barrier((held, out_weight))

    def next_chip(at):
        z = (2 * at["zh"] + at["zl"] + (1 if at["core"] == 0 else -1)) % 8
        return {"zh": z // 2, "zl": z % 2}

    beside = permute(weight, ("zl", "core", "zh"), next_chip)
    own_q, own_kv = held[:, : PART + EXTRA], held[:, PART:]
    after, before = ring(own_kv, "y", -1), ring(own_kv, "y", 1)
    keys_values = [own_kv, after, ring(after, "y", -1), before]
    q_before = ring(own_q, "x", 1)
    queries = [own_q, ring(own_q, "x", -1), ring(q_before, "x", 1), q_before]
    pieces = attend(queries, keys_values)
    pieces = [pieces[0]] + [ring(pieces[s], "x", OFFSETS[s]) for s in (1, 3, 2)]
    attended = combine(pieces).reshape(8, PART, HD)
    heads = lax.all_to_all(attended, ("zh", "zl"), 0, 0, tiled=True)
    mixed = project(heads, out_weight, beside)
    other = permute(mixed[HALF:], ("core",), lambda at: {"core": at["core"] + 1})
    return (mixed[:HALF].astype(jnp.float32) + other.astype(jnp.float32)).astype(jnp.bfloat16)[None]


def solution(mesh):
    apart = Mesh(mesh.devices.reshape(tuple(SIZES.values())), AXES)
    block, head = ("zh", "y", "x"), ("zl", "core")
    array = P(block, head, None, None)
    return jax.shard_map(
        body,
        mesh=apart,
        in_specs=(array, array, array, P(block), P(head, None)),
        out_specs=P(block, head, None),
        check_vma=False,
    )
```

time: 113 us -> 93.5 us (0.83)
  the two profiles are of different devices: /device:TPU:6 before, /device:TPU:1 now
where the time goes in v2:
time: 93.5 us; the launch traced here: 94 us
  blocking collectives  38.8 us (41%)
  starting transfers between devices  24 us (26%)
  waiting for transfers between devices  17 us (18%)
  Pallas kernels  9.56 us (10%)
  local copies, waits for them, and re-layouts  2.83 us (3%)
  other arithmetic  1.67 us (2%)
    all_to_all x1, blocking collectives, body(): held = lax.all_to_all(sent, ('zh', 'zl'), 0, 0, tiled=True)  25 us
    ppermute x12, starting transfers between devices, permute(): return lax.ppermute(array, tuple(axes), pairs)  24 us
    ppermute x12, waiting for transfers between devices, permute(): return lax.ppermute(array, tuple(axes), pairs)  17 us
    all_to_all x1, blocking collectives, body(): heads = lax.all_to_all(attended, ('zh', 'zl'), 0, 0, tiled=True)  13.8 us
    pallas_call x1, Pallas kernels, attend(): pl.pallas_call(attention_kernel, out_shape=jax.ShapeDtypeStruct((4, HD +...  7.37 us
    dynamic_slice x8, local copies, waits for them, and re-layouts, heads_of(): array = lax.dynamic_index_in_dim(array, c, 2, keepdims=False)  2.59 us
    pallas_call x1, Pallas kernels, project(): pl.pallas_call(project_kernel, out_shape=jax.ShapeDtypeStruct((PART, own....  1.92 us
  transfers between devices with their start and end apart: 12, of which 8 were waited for; matrix products, arithmetic and copies ran while one was open for 1% of the time, Pallas kernels for 8%

profile of v2, /device:TPU:1, one launch (start us, length us, event | category | flops | bytes accessed | tf_op | source)
XLA Modules:
  0.0 94.0 jit_solution(7056316552878477610)
XLA Ops:
  0.0 0.0 copy-start
  0.0 1.2 %constant_dynamic-slice_fusion.4 = (bf16[48,2,1,4,128]{4,3,2,1,0:T(4,128)(2,1)S(1)}, bf16[48,2,1,4,128]{4,3,2,1,0:T(4,128)(2,1)S(1)}) fusion(bf16[48,2,2,4,128]{4,3,2,1,0:T(4,128)(2,1)} %bitcast.63, s32[]{:T(128)S(6)} %select_n.12, s32[]{:T(128)S(6)} %select_n.11), kind=kLoop, calls=%fused_computation.23 | loop fusion | bytes 393224 | tf_op jit(solution)/shard_map/jit(dynamic_index_in_dim)/dynamic_slice | solution.py:331
  1.2 1.3 %constant_dynamic-slice_fusion = (bf16[48,2,1,4,128]{4,3,2,1,0:T(4,128)(2,1)S(1)}, bf16[48,2,1,4,128]{4,3,2,1,0:T(4,128)(2,1)S(1)}, bf16[48,2,1,4,128]{4,3,2,1,0:T(4,128)(2,1)S(1)}, bf16[48,2,1,4,128]{4,3,2,1,0:T(4,128)(2,1)S(1)}) fusion(bf16[48,2,2,4,128]{4,3,2,1,0:T(4,128)(2,1)} %bitcast.64, s32[]{:T(128)S(6)} %select_n.11, s32[]{:T(128)S(6)} %select_n.12, ...), kind=kLoop, calls=%fused_computation.19 | loop fusion | bytes 786440 | tf_op jit(solution)/shard_map/jit(dynamic_index_in_dim)/dynamic_slice | solution.py:331
  2.6 3.3 %collective-permute-start = (bf16[8,3,48,128]{3,2,0,1:T(8,128)(2,1)S(1)}, bf16[8,3,48,128]{3,2,0,1:T(8,128)(2,1)S(1)}, u32[]{:S(2)}, u32[]{:S(2)}) collective-permute-start(bf16[8,3,48,128]{3,2,0,1:T(8,128)(2,1)S(1)} %pad_maximum_fusion), channel_id=1, source_target_pairs={{0,64},{64,0},{1,65},{65,1},{2,66},{66,2},{3,67},{67,3},{4,68},{68... | collective-permute-start | bytes 884744 | tf_op jit(solution)/shard_map/ppermute | solution.py:40
  6.0 0.8 convert_reduce_fusion
  6.8 0.3 collective-permute-done
  7.3 25.0 %all_to_all.10 = bf16[8,304,128]{2,1,0:T(8,128)(2,1)S(1)} all-to-all(bf16[8,304,128]{2,1,0:T(8,128)(2,1)S(1)} %fusion.1), channel_id=1, replica_groups=mesh['zl'=2,'core'=2,'zh'=4,'y'=4,'x'=4] {'zh','zl'}, dimensions={0} | all-to-all | bytes 1245184 | tf_op jit(solution)/shard_map/all_to_all | solution.py:343
  32.3 0.0 copy-done
  32.3 0.0 collective-permute-start.10
  32.3 2.6 %collective-permute-start.4 = (bf16[8,208,128]{2,1,0:T(8,128)(2,1)S(1)}, bf16[8,208,128]{2,1,0:T(8,128)(2,1)S(1)}, u32[]{:S(2)}, u32[]{:S(2)}) collective-permute-start(bf16[8,208,128]{2,1,0:T(8,128)(2,1)S(1)} %slice.37.refs_4_), channel_id=1, source_target_pairs={{0,12},{1,13},{2,14},{3,15},{4,0},{5,1},{6,2},{7,3},{8,4},{9,5},{1... | collective-permute-start | bytes 1277960 | tf_op jit(solution)/shard_map/ppermute | solution.py:40
  34.9 1.4 %collective-permute-start.2 = (bf16[8,112,128]{2,1,0:T(8,128)(2,1)S(1)}, bf16[8,112,128]{2,1,0:T(8,128)(2,1)S(1)}, u32[]{:S(2)}, u32[]{:S(2)}) collective-permute-start(bf16[8,112,128]{2,1,0:T(8,128)(2,1)S(1)} %slice.36.refs_0_), channel_id=1, source_target_pairs={{0,1},{1,2},{2,3},{3,0},{4,5},{5,6},{6,7},{7,4},{8,9},{9,10},{10,1... | collective-permute-start | bytes 688136 | tf_op jit(solution)/shard_map/ppermute | solution.py:40
  36.3 0.0 collective-permute-start.6
  36.3 3.7 %collective-permute-done.4.refs_5_ = bf16[8,208,128]{2,1,0:T(8,128)(2,1)S(1)} collective-permute-done((bf16[8,208,128]{2,1,0:T(8,128)(2,1)S(1)}, bf16[8,208,128]{2,1,0:T(8,128)(2,1)S(1)}, u32[]{:S(2)}, u32[]{:S(2)}) %collective-permute-start.4) | collective-permute-done | bytes 426016 | tf_op jit(solution)/shard_map/ppermute | solution.py:40
  39.9 3.4 %collective-permute-start.5 = (bf16[8,208,128]{2,1,0:T(8,128)(2,1)S(1)}, bf16[8,208,128]{2,1,0:T(8,128)(2,1)S(1)}, u32[]{:S(2)}, u32[]{:S(2)}) collective-permute-start(bf16[8,208,128]{2,1,0:T(8,128)(2,1)S(1)} %collective-permute-done.4.refs_5_), channel_id=1, source_target_pairs={{0,12},{1,13},{2,14},{3,15},{4,0},{5,1},{6,2},{7,3},{8,4},{9,5},{1... | collective-permute-start | bytes 1277960 | tf_op jit(solution)/shard_map/ppermute | solution.py:40
  43.4 2.7 %collective-permute-start.1 = (bf16[8,112,128]{2,1,0:T(8,128)(2,1)S(1)}, bf16[8,112,128]{2,1,0:T(8,128)(2,1)S(1)}, u32[]{:S(2)}, u32[]{:S(2)}) collective-permute-start(bf16[8,112,128]{2,1,0:T(8,128)(2,1)S(1)} %slice.36.refs_0_), channel_id=1, source_target_pairs={{0,3},{1,0},{2,1},{3,2},{4,7},{5,4},{6,5},{7,6},{8,11},{9,8},{10,9... | collective-permute-start | bytes 688136 | tf_op jit(solution)/shard_map/ppermute | solution.py:40
  46.1 0.0 collective-permute-done.2.refs_3_
  46.1 0.0 collective-permute-start.3
  46.1 4.4 %collective-permute-done.1.refs_1_ = bf16[8,112,128]{2,1,0:T(8,128)(2,1)S(1)} collective-permute-done((bf16[8,112,128]{2,1,0:T(8,128)(2,1)S(1)}, bf16[8,112,128]{2,1,0:T(8,128)(2,1)S(1)}, u32[]{:S(2)}, u32[]{:S(2)}) %collective-permute-start.1) | collective-permute-done | bytes 229408 | tf_op jit(solution)/shard_map/ppermute | solution.py:40
  50.5 0.0 collective-permute-done.6.refs_7_
  50.5 1.9 %collective-permute-done.3.refs_2_ = bf16[8,112,128]{2,1,0:T(8,128)(2,1)S(1)} collective-permute-done((bf16[8,112,128]{2,1,0:T(8,128)(2,1)S(1)}, bf16[8,112,128]{2,1,0:T(8,128)(2,1)S(1)}, u32[]{:S(2)}, u32[]{:S(2)}) %collective-permute-start.3) | collective-permute-done | bytes 229408 | tf_op jit(solution)/shard_map/ppermute | solution.py:40
  52.5 0.0 collective-permute-done.5.refs_6_
  52.5 7.4 %shard_map.55 = bf16[4,144,768]{2,1,0:T(8,128)(2,1)S(1)} custom-call(bf16[8,112,128]{2,1,0:T(8,128)(2,1)S(1)} %slice.36.refs_0_, bf16[8,112,128]{2,1,0:T(8,128)(2,1)S(1)} %collective-permute-done.1.refs_1_, bf16[8,112,128]{2,1,0:T(8,128)(2,1)S(1)} %collective-permute-done.3.refs_2_, bf16[8,112,128]{2,1,0:T(8,128)(2,1)S(1)} %collective-permute-done.2.refs_3_, ...), custom_call_target="tpu_custom_call" | custom-call | tf_op jit(solution)/shard_map/pallas_call | solution.py:273
  59.9 0.1 slice_bitcast_fusion
  59.9 2.6 %collective-permute-start.9 = (bf16[144,768]{1,0:T(8,128)(2,1)S(1)}, bf16[144,768]{1,0:T(8,128)(2,1)S(1)}, u32[]{:S(2)}, u32[]{:S(2)}) collective-permute-start(bf16[144,768]{1,0:T(8,128)(2,1)S(1)} %get-tuple-element.9), channel_id=1, source_target_pairs={{0,2},{1,3},{2,0},{3,1},{4,6},{5,7},{6,4},{7,5},{8,10},{9,11},{10,... | collective-permute-start | bytes 663560 | tf_op jit(solution)/shard_map/ppermute | solution.py:40
  62.5 0.5 collective-permute-start.8
  63.0 1.0 %collective-permute-start.7 = (bf16[144,768]{1,0:T(8,128)(2,1)S(1)}, bf16[144,768]{1,0:T(8,128)(2,1)S(1)}, u32[]{:S(2)}, u32[]{:S(2)}) collective-permute-start(bf16[144,768]{1,0:T(8,128)(2,1)S(1)} %get-tuple-element.11), channel_id=1, source_target_pairs={{0,1},{1,2},{2,3},{3,0},{4,5},{5,6},{6,7},{7,4},{8,9},{9,10},{10,1... | collective-permute-start | bytes 663560 | tf_op jit(solution)/shard_map/ppermute | solution.py:40
  64.0 2.3 %collective-permute-done.9.refs_3_ = bf16[144,768]{1,0:T(8,128)(2,1)S(1)} collective-permute-done((bf16[144,768]{1,0:T(8,128)(2,1)S(1)}, bf16[144,768]{1,0:T(8,128)(2,1)S(1)}, u32[]{:S(2)}, u32[]{:S(2)}) %collective-permute-start.9) | collective-permute-done | bytes 221216 | tf_op jit(solution)/shard_map/ppermute | solution.py:40
  66.3 2.3 %collective-permute-done.8.refs_2_ = bf16[144,768]{1,0:T(8,128)(2,1)S(1)} collective-permute-done((bf16[144,768]{1,0:T(8,128)(2,1)S(1)}, bf16[144,768]{1,0:T(8,128)(2,1)S(1)}, u32[]{:S(2)}, u32[]{:S(2)}) %collective-permute-start.8) | collective-permute-done | bytes 221216 | tf_op jit(solution)/shard_map/ppermute | solution.py:40
  68.6 0.7 collective-permute-done.7.refs_1_
  69.3 0.3 shard_map.56
  69.5 13.8 %all_to_all.11.heads_ref = bf16[8,96,128]{2,1,0:T(8,128)(2,1)S(1)} all-to-all(bf16[8,96,128]{2,1,0:T(8,128)(2,1)S(1)} %bitcast.56), channel_id=1, replica_groups=mesh['zl'=2,'core'=2,'zh'=4,'y'=4,'x'=4] {'zh','zl'}, dimensions={0} | all-to-all | bytes 393216 | tf_op jit(solution)/shard_map/all_to_all | solution.py:359
  83.4 0.0 collective-permute-done.10.beside_ref
  83.4 1.9 %shard_map.57 = bf16[96,4096]{1,0:T(8,128)(2,1)S(1)} custom-call(bf16[8,96,128]{2,1,0:T(8,128)(2,1)S(1)} %all_to_all.11.heads_ref, bf16[512,4096]{1,0:T(8,128)(2,1)S(1)} %copy-done, bf16[512,4096]{1,0:T(8,128)(2,1)S(1)} %collective-permute-done.10.beside_ref), custom_call_target="tpu_custom_call" | custom-call | tf_op jit(solution)/shard_map/pallas_call | solution.py:316
  85.3 6.5 %collective-permute-start.11 = (bf16[48,4096]{1,0:T(8,128)(2,1)S(1)}, bf16[48,4096]{1,0:T(8,128)(2,1)S(1)}, u32[]{:S(2)}, u32[]{:S(2)}) collective-permute-start(bf16[48,4096]{1,0:T(8,128)(2,1)S(1)} %slice.52), channel_id=1, source_target_pairs={{0,64},{64,0},{1,65},{65,1},{2,66},{66,2},{3,67},{67,3},{4,68},{68... | collective-permute-start | bytes 1179656 | tf_op jit(solution)/shard_map/ppermute | solution.py:40
  91.8 1.3 %collective-permute-done.11 = bf16[48,4096]{1,0:T(8,128)(2,1)S(1)} collective-permute-done((bf16[48,4096]{1,0:T(8,128)(2,1)S(1)}, bf16[48,4096]{1,0:T(8,128)(2,1)S(1)}, u32[]{:S(2)}, u32[]{:S(2)}) %collective-permute-start.11) | collective-permute-done | bytes 393248 | tf_op jit(solution)/shard_map/ppermute | solution.py:40
  93.2 0.8 fusion
  (18 shorter events, 0.3 us)
Async XLA Ops:
  0.0 32.3 %copy-start = (bf16[512,4096]{1,0:T(8,128)(2,1)S(1)}, bf16[512,4096]{1,0:T(8,128)(2,1)}, u32[]{:S(2)}) copy-start(bf16[512,4096]{1,0:T(8,128)(2,1)} %own_ref.1) | copy-start | bytes 12582916
  2.6 4.5 %collective-permute-start = (bf16[8,3,48,128]{3,2,0,1:T(8,128)(2,1)S(1)}, bf16[8,3,48,128]{3,2,0,1:T(8,128)(2,1)S(1)}, u32[]{:S(2)}, u32[]{:S(2)}) collective-permute-start(bf16[8,3,48,128]{3,2,0,1:T(8,128)(2,1)S(1)} %pad_maximum_fusion), channel_id=1, source_target_pairs={{0,64},{64,0},{1,65},{65,1},{2,66},{66,2},{3,67},{67,3},{4,68},{68... | collective-permute-start | bytes 884744 | tf_op jit(solution)/shard_map/ppermute | solution.py:40
  32.3 51.1 %collective-permute-start.10 = (bf16[512,4096]{1,0:T(8,128)(2,1)S(1)}, bf16[512,4096]{1,0:T(8,128)(2,1)S(1)}, u32[]{:S(2)}, u32[]{:S(2)}) collective-permute-start(bf16[512,4096]{1,0:T(8,128)(2,1)S(1)} %copy-done), channel_id=1, source_target_pairs={{0,128},{16,144},{32,160},{48,176},{64,240},{80,192},{96,208},{112... | collective-permute-start | bytes 12582920 | tf_op jit(solution)/shard_map/ppermute | solution.py:40
  32.3 7.6 %collective-permute-start.4 = (bf16[8,208,128]{2,1,0:T(8,128)(2,1)S(1)}, bf16[8,208,128]{2,1,0:T(8,128)(2,1)S(1)}, u32[]{:S(2)}, u32[]{:S(2)}) collective-permute-start(bf16[8,208,128]{2,1,0:T(8,128)(2,1)S(1)} %slice.37.refs_4_), channel_id=1, source_target_pairs={{0,12},{1,13},{2,14},{3,15},{4,0},{5,1},{6,2},{7,3},{8,4},{9,5},{1... | collective-permute-start | bytes 1277960 | tf_op jit(solution)/shard_map/ppermute | solution.py:40
  34.9 11.2 %collective-permute-start.2 = (bf16[8,112,128]{2,1,0:T(8,128)(2,1)S(1)}, bf16[8,112,128]{2,1,0:T(8,128)(2,1)S(1)}, u32[]{:S(2)}, u32[]{:S(2)}) collective-permute-start(bf16[8,112,128]{2,1,0:T(8,128)(2,1)S(1)} %slice.36.refs_0_), channel_id=1, source_target_pairs={{0,1},{1,2},{2,3},{3,0},{4,5},{5,6},{6,7},{7,4},{8,9},{9,10},{10,1... | collective-permute-start | bytes 688136 | tf_op jit(solution)/shard_map/ppermute | solution.py:40
  36.3 14.3 %collective-permute-start.6 = (bf16[8,208,128]{2,1,0:T(8,128)(2,1)S(1)}, bf16[8,208,128]{2,1,0:T(8,128)(2,1)S(1)}, u32[]{:S(2)}, u32[]{:S(2)}) collective-permute-start(bf16[8,208,128]{2,1,0:T(8,128)(2,1)S(1)} %slice.37.refs_4_), channel_id=1, source_target_pairs={{0,4},{1,5},{2,6},{3,7},{4,8},{5,9},{6,10},{7,11},{8,12},{9,13},{1... | collective-permute-start | bytes 1277960 | tf_op jit(solution)/shard_map/ppermute | solution.py:40
  39.9 12.5 %collective-permute-start.5 = (bf16[8,208,128]{2,1,0:T(8,128)(2,1)S(1)}, bf16[8,208,128]{2,1,0:T(8,128)(2,1)S(1)}, u32[]{:S(2)}, u32[]{:S(2)}) collective-permute-start(bf16[8,208,128]{2,1,0:T(8,128)(2,1)S(1)} %collective-permute-done.4.refs_5_), channel_id=1, source_target_pairs={{0,12},{1,13},{2,14},{3,15},{4,0},{5,1},{6,2},{7,3},{8,4},{9,5},{1... | collective-permute-start | bytes 1277960 | tf_op jit(solution)/shard_map/ppermute | solution.py:40
  43.4 7.2 %collective-permute-start.1 = (bf16[8,112,128]{2,1,0:T(8,128)(2,1)S(1)}, bf16[8,112,128]{2,1,0:T(8,128)(2,1)S(1)}, u32[]{:S(2)}, u32[]{:S(2)}) collective-permute-start(bf16[8,112,128]{2,1,0:T(8,128)(2,1)S(1)} %slice.36.refs_0_), channel_id=1, source_target_pairs={{0,3},{1,0},{2,1},{3,2},{4,7},{5,4},{6,5},{7,6},{8,11},{9,8},{10,9... | collective-permute-start | bytes 688136 | tf_op jit(solution)/shard_map/ppermute | solution.py:40
  46.1 6.4 %collective-permute-start.3 = (bf16[8,112,128]{2,1,0:T(8,128)(2,1)S(1)}, bf16[8,112,128]{2,1,0:T(8,128)(2,1)S(1)}, u32[]{:S(2)}, u32[]{:S(2)}) collective-permute-start(bf16[8,112,128]{2,1,0:T(8,128)(2,1)S(1)} %collective-permute-done.2.refs_3_), channel_id=1, source_target_pairs={{0,1},{1,2},{2,3},{3,0},{4,5},{5,6},{6,7},{7,4},{8,9},{9,10},{10,1... | collective-permute-start | bytes 688136 | tf_op jit(solution)/shard_map/ppermute | solution.py:40
  59.9 6.4 %collective-permute-start.9 = (bf16[144,768]{1,0:T(8,128)(2,1)S(1)}, bf16[144,768]{1,0:T(8,128)(2,1)S(1)}, u32[]{:S(2)}, u32[]{:S(2)}) collective-permute-start(bf16[144,768]{1,0:T(8,128)(2,1)S(1)} %get-tuple-element.9), channel_id=1, source_target_pairs={{0,2},{1,3},{2,0},{3,1},{4,6},{5,7},{6,4},{7,5},{8,10},{9,11},{10,... | collective-permute-start | bytes 663560 | tf_op jit(solution)/shard_map/ppermute | solution.py:40
  62.5 6.0 %collective-permute-start.8 = (bf16[144,768]{1,0:T(8,128)(2,1)S(1)}, bf16[144,768]{1,0:T(8,128)(2,1)S(1)}, u32[]{:S(2)}, u32[]{:S(2)}) collective-permute-start(bf16[144,768]{1,0:T(8,128)(2,1)S(1)} %get-tuple-element.10), channel_id=1, source_target_pairs={{0,3},{1,0},{2,1},{3,2},{4,7},{5,4},{6,5},{7,6},{8,11},{9,8},{10,9... | collective-permute-start | bytes 663560 | tf_op jit(solution)/shard_map/ppermute | solution.py:40
  63.0 6.3 %collective-permute-start.7 = (bf16[144,768]{1,0:T(8,128)(2,1)S(1)}, bf16[144,768]{1,0:T(8,128)(2,1)S(1)}, u32[]{:S(2)}, u32[]{:S(2)}) collective-permute-start(bf16[144,768]{1,0:T(8,128)(2,1)S(1)} %get-tuple-element.11), channel_id=1, source_target_pairs={{0,1},{1,2},{2,3},{3,0},{4,5},{5,6},{6,7},{7,4},{8,9},{9,10},{10,1... | collective-permute-start | bytes 663560 | tf_op jit(solution)/shard_map/ppermute | solution.py:40
  85.3 7.9 %collective-permute-start.11 = (bf16[48,4096]{1,0:T(8,128)(2,1)S(1)}, bf16[48,4096]{1,0:T(8,128)(2,1)S(1)}, u32[]{:S(2)}, u32[]{:S(2)}) collective-permute-start(bf16[48,4096]{1,0:T(8,128)(2,1)S(1)} %slice.52), channel_id=1, source_target_pairs={{0,64},{64,0},{1,65},{65,1},{2,66},{66,2},{3,67},{67,3},{4,68},{68... | collective-permute-start | bytes 1179656 | tf_op jit(solution)/shard_map/ppermute | solution.py:40

commit v3 on v2

--- a/solution.py
+++ b/solution.py
@@ -247,7 +247,7 @@
 
 
 def project_kernel(heads_ref, own_ref, beside_ref, out_ref, held):
-    zl, tile = at_spot()[0], 1024
+    zl, tile = at_spot()[0], 2048
     for zh in range(4):
         columns = slice(zh * HD, (zh + 1) * HD)
         held[0, :, columns] = heads_ref[2 * zh + zl]
@@ -336,9 +336,9 @@
     theirs = permute(theirs, ("core",), lambda at: {"core": at["core"] + 1})
     marks = jnp.arange(8, dtype=jnp.int32)
     counts = jnp.sum((doc_ids[None, :] < marks[:, None]).astype(jnp.float32), axis=1).astype(jnp.bfloat16)
-    extra = jnp.broadcast_to(jnp.pad(counts, (0, HD - 8)), (8, EXTRA, HD))
+    extra = jnp.broadcast_to(jnp.pad(counts, (0, HD - 8)), (8, EXTRA // 2, HD))
     sent = jnp.concatenate(
-        [mine[0], theirs[:, 0], extra, mine[1], theirs[:, 1], mine[2], theirs[:, 2]], axis=1
+        [mine[0], theirs[:, 0], mine[1], theirs[:, 1], mine[2], theirs[:, 2], extra], axis=1
     )
     held = lax.all_to_all(sent, ("zh", "zl"), 0, 0, tiled=True)
     held, weight = lax.optimization_barrier((held, out_weight))
@@ -348,7 +348,9 @@
         return {"zh": z // 2, "zl": z % 2}
 
     beside = permute(weight, ("zl", "core", "zh"), next_chip)
-    own_q, own_kv = held[:, : PART + EXTRA], held[:, PART:]
+    extra = jnp.concatenate([held[:, 3 * PART :]] * 2, axis=1)
+    own_q = jnp.concatenate([held[:, :PART], extra], axis=1)
+    own_kv = jnp.concatenate([extra, held[:, PART : 3 * PART]], axis=1)
     after, before = ring(own_kv, "y", -1), ring(own_kv, "y", 1)
     keys_values = [own_kv, after, ring(after, "y", -1), before]
     q_before = ring(own_q, "x", 1)

time: 93.5 us -> 92.9 us (level); the launches traced: 94 us -> 92 us
  starting transfers between devices: 24 us -> 19.9 us
  waiting for transfers between devices: 17 us -> 19.1 us
  blocking collectives: 38.8 us -> 36.8 us
  Pallas kernels: 9.56 us -> 11.5 us
    ppermute x12, starting transfers between devices: 24 us -> 19.9 us  [permute(): return lax.ppermute(array, tuple(axes), pairs)]
    pallas_call x1, Pallas kernels: 7.37 us -> 9.58 us  [attend(): pl.pallas_call(attention_kernel, out_shape=jax.ShapeDtypeStruct((4, HD +...]
    ppermute x12, waiting for transfers between devices: 17 us -> 19.1 us  [permute(): return lax.ppermute(array, tuple(axes), pairs)]
    all_to_all x1, blocking collectives: 13.8 us -> 11.9 us  [body(): heads = lax.all_to_all(attended, ('zh', 'zl'), 0, 0, tiled=True)]
  transfers between devices with their start and end apart: 12 -> 12, of which waited for: 8 -> 7; matrix products, arithmetic and copies ran while one was open for 1% -> 1% of each run, Pallas kernels for 8% -> 11%
where the time goes in v3:
time: 92.9 us; the launch traced here: 92 us
  blocking collectives  36.8 us (40%)
  starting transfers between devices  19.9 us (21%)
  waiting for transfers between devices  19.1 us (21%)
  Pallas kernels  11.5 us (12%)
  local copies, waits for them, and re-layouts  2.83 us (3%)
  other arithmetic  1.73 us (2%)
    all_to_all x1, blocking collectives, body(): held = lax.all_to_all(sent, ('zh', 'zl'), 0, 0, tiled=True)  24.9 us
    ppermute x12, starting transfers between devices, permute(): return lax.ppermute(array, tuple(axes), pairs)  19.9 us
    ppermute x12, waiting for transfers between devices, permute(): return lax.ppermute(array, tuple(axes), pairs)  19.1 us
    all_to_all x1, blocking collectives, body(): heads = lax.all_to_all(attended, ('zh', 'zl'), 0, 0, tiled=True)  11.9 us
    pallas_call x1, Pallas kernels, attend(): pl.pallas_call(attention_kernel, out_shape=jax.ShapeDtypeStruct((4, HD +...  9.58 us
    dynamic_slice x8, local copies, waits for them, and re-layouts, heads_of(): array = lax.dynamic_index_in_dim(array, c, 2, keepdims=False)  2.59 us
  transfers between devices with their start and end apart: 12, of which 7 were waited for; matrix products, arithmetic and copies ran while one was open for 1% of the time, Pallas kernels for 11%

profile of v3, /device:TPU:1, one launch (start us, length us, event | category | flops | bytes accessed | tf_op | source)
XLA Modules:
  0.0 92.0 jit_solution(8061537683587721973)
XLA Ops:
  0.0 0.0 copy-start
  0.0 1.2 %constant_dynamic-slice_fusion.4 = (bf16[48,2,1,4,128]{4,3,2,1,0:T(4,128)(2,1)S(1)}, bf16[48,2,1,4,128]{4,3,2,1,0:T(4,128)(2,1)S(1)}) fusion(bf16[48,2,2,4,128]{4,3,2,1,0:T(4,128)(2,1)} %bitcast.63, s32[]{:T(128)S(6)} %select_n.12, s32[]{:T(128)S(6)} %select_n.11), kind=kLoop, calls=%fused_computation.25 | loop fusion | bytes 393224 | tf_op jit(solution)/shard_map/jit(dynamic_index_in_dim)/dynamic_slice | solution.py:331
  1.2 1.3 %constant_dynamic-slice_fusion = (bf16[48,2,1,4,128]{4,3,2,1,0:T(4,128)(2,1)S(1)}, bf16[48,2,1,4,128]{4,3,2,1,0:T(4,128)(2,1)S(1)}, bf16[48,2,1,4,128]{4,3,2,1,0:T(4,128)(2,1)S(1)}, bf16[48,2,1,4,128]{4,3,2,1,0:T(4,128)(2,1)S(1)}) fusion(bf16[48,2,2,4,128]{4,3,2,1,0:T(4,128)(2,1)} %bitcast.64, s32[]{:T(128)S(6)} %select_n.11, s32[]{:T(128)S(6)} %select_n.12, ...), kind=kLoop, calls=%fused_computation.21 | loop fusion | bytes 786440 | tf_op jit(solution)/shard_map/jit(dynamic_index_in_dim)/dynamic_slice | solution.py:331
  2.6 3.3 %collective-permute-start = (bf16[8,3,48,128]{3,2,0,1:T(8,128)(2,1)S(1)}, bf16[8,3,48,128]{3,2,0,1:T(8,128)(2,1)S(1)}, u32[]{:S(2)}, u32[]{:S(2)}) collective-permute-start(bf16[8,3,48,128]{3,2,0,1:T(8,128)(2,1)S(1)} %pad_maximum_fusion.1), channel_id=1, source_target_pairs={{0,64},{64,0},{1,65},{65,1},{2,66},{66,2},{3,67},{67,3},{4,68},{68... | collective-permute-start | bytes 884744 | tf_op jit(solution)/shard_map/ppermute | solution.py:40
  6.0 0.8 convert_reduce_fusion
  6.8 0.3 collective-permute-done
  7.3 24.9 %all_to_all.10 = bf16[8,296,128]{2,1,0:T(8,128)(2,1)S(1)} all-to-all(bf16[8,296,128]{2,1,0:T(8,128)(2,1)S(1)} %constant_dynamic-update-slice_fusion), channel_id=1, replica_groups=mesh['zl'=2,'core'=2,'zh'=4,'y'=4,'x'=4] {'zh','zl'}, dimensions={0} | all-to-all | bytes 1212416 | tf_op jit(solution)/shard_map/all_to_all | solution.py:343
  32.2 0.0 copy-done
  32.2 0.0 collective-permute-start.10
  32.3 2.6 %collective-permute-start.4 = (bf16[8,208,128]{2,1,0:T(8,128)(2,1)S(1)}, bf16[8,208,128]{2,1,0:T(8,128)(2,1)S(1)}, u32[]{:S(2)}, u32[]{:S(2)}) collective-permute-start(bf16[8,208,128]{2,1,0:T(8,128)(2,1)S(1)} %pad_maximum_fusion.refs_4_), channel_id=1, source_target_pairs={{0,12},{1,13},{2,14},{3,15},{4,0},{5,1},{6,2},{7,3},{8,4},{9,5},{1... | collective-permute-start | bytes 1277960 | tf_op jit(solution)/shard_map/ppermute | solution.py:40
  34.9 1.4 %collective-permute-start.2 = (bf16[8,112,128]{2,1,0:T(8,128)(2,1)S(1)}, bf16[8,112,128]{2,1,0:T(8,128)(2,1)S(1)}, u32[]{:S(2)}, u32[]{:S(2)}) collective-permute-start(bf16[8,112,128]{2,1,0:T(8,128)(2,1)S(1)} %pad_maximum_fusion.2.refs_0_), channel_id=1, source_target_pairs={{0,1},{1,2},{2,3},{3,0},{4,5},{5,6},{6,7},{7,4},{8,9},{9,10},{10,1... | collective-permute-start | bytes 688136 | tf_op jit(solution)/shard_map/ppermute | solution.py:40
  36.2 0.0 collective-permute-start.6
  36.2 3.7 %collective-permute-done.4.refs_5_ = bf16[8,208,128]{2,1,0:T(8,128)(2,1)S(1)} collective-permute-done((bf16[8,208,128]{2,1,0:T(8,128)(2,1)S(1)}, bf16[8,208,128]{2,1,0:T(8,128)(2,1)S(1)}, u32[]{:S(2)}, u32[]{:S(2)}) %collective-permute-start.4) | collective-permute-done | bytes 426016 | tf_op jit(solution)/shard_map/ppermute | solution.py:40
  39.9 3.4 %collective-permute-start.5 = (bf16[8,208,128]{2,1,0:T(8,128)(2,1)S(1)}, bf16[8,208,128]{2,1,0:T(8,128)(2,1)S(1)}, u32[]{:S(2)}, u32[]{:S(2)}) collective-permute-start(bf16[8,208,128]{2,1,0:T(8,128)(2,1)S(1)} %collective-permute-done.4.refs_5_), channel_id=1, source_target_pairs={{0,12},{1,13},{2,14},{3,15},{4,0},{5,1},{6,2},{7,3},{8,4},{9,5},{1... | collective-permute-start | bytes 1277960 | tf_op jit(solution)/shard_map/ppermute | solution.py:40
  43.3 2.7 %collective-permute-start.1 = (bf16[8,112,128]{2,1,0:T(8,128)(2,1)S(1)}, bf16[8,112,128]{2,1,0:T(8,128)(2,1)S(1)}, u32[]{:S(2)}, u32[]{:S(2)}) collective-permute-start(bf16[8,112,128]{2,1,0:T(8,128)(2,1)S(1)} %pad_maximum_fusion.2.refs_0_), channel_id=1, source_target_pairs={{0,3},{1,0},{2,1},{3,2},{4,7},{5,4},{6,5},{7,6},{8,11},{9,8},{10,9... | collective-permute-start | bytes 688136 | tf_op jit(solution)/shard_map/ppermute | solution.py:40
  46.0 0.0 collective-permute-done.2.refs_3_
  46.0 0.0 collective-permute-start.3
  46.0 4.6 %collective-permute-done.1.refs_1_ = bf16[8,112,128]{2,1,0:T(8,128)(2,1)S(1)} collective-permute-done((bf16[8,112,128]{2,1,0:T(8,128)(2,1)S(1)}, bf16[8,112,128]{2,1,0:T(8,128)(2,1)S(1)}, u32[]{:S(2)}, u32[]{:S(2)}) %collective-permute-start.1) | collective-permute-done | bytes 229408 | tf_op jit(solution)/shard_map/ppermute | solution.py:40
  50.6 0.0 collective-permute-done.6.refs_7_
  50.6 1.8 %collective-permute-done.3.refs_2_ = bf16[8,112,128]{2,1,0:T(8,128)(2,1)S(1)} collective-permute-done((bf16[8,112,128]{2,1,0:T(8,128)(2,1)S(1)}, bf16[8,112,128]{2,1,0:T(8,128)(2,1)S(1)}, u32[]{:S(2)}, u32[]{:S(2)}) %collective-permute-start.3) | collective-permute-done | bytes 229408 | tf_op jit(solution)/shard_map/ppermute | solution.py:40
  52.4 0.0 collective-permute-done.5.refs_6_
  52.4 9.6 %shard_map.55 = bf16[4,144,768]{2,1,0:T(8,128)(2,1)S(1)} custom-call(bf16[8,112,128]{2,1,0:T(8,128)(2,1)S(1)} %pad_maximum_fusion.2.refs_0_, bf16[8,112,128]{2,1,0:T(8,128)(2,1)S(1)} %collective-permute-done.1.refs_1_, bf16[8,112,128]{2,1,0:T(8,128)(2,1)S(1)} %collective-permute-done.3.refs_2_, bf16[8,112,128]{2,1,0:T(8,128)(2,1)S(1)} %collective-permute-done.2.refs_3_, ...), custom_call_target="tpu_custom_call" | custom-call | tf_op jit(solution)/shard_map/pallas_call | solution.py:273
  62.0 0.1 slice_bitcast_fusion
  62.1 0.1 collective-permute-start.9
  62.2 1.5 %collective-permute-start.8 = (bf16[144,768]{1,0:T(8,128)(2,1)S(1)}, bf16[144,768]{1,0:T(8,128)(2,1)S(1)}, u32[]{:S(2)}, u32[]{:S(2)}) collective-permute-start(bf16[144,768]{1,0:T(8,128)(2,1)S(1)} %get-tuple-element.10), channel_id=1, source_target_pairs={{0,3},{1,0},{2,1},{3,2},{4,7},{5,4},{6,5},{7,6},{8,11},{9,8},{10,9... | collective-permute-start | bytes 663560 | tf_op jit(solution)/shard_map/ppermute | solution.py:40
  63.6 0.1 collective-permute-start.7
  63.7 4.8 %collective-permute-done.9.refs_3_ = bf16[144,768]{1,0:T(8,128)(2,1)S(1)} collective-permute-done((bf16[144,768]{1,0:T(8,128)(2,1)S(1)}, bf16[144,768]{1,0:T(8,128)(2,1)S(1)}, u32[]{:S(2)}, u32[]{:S(2)}) %collective-permute-start.9) | collective-permute-done | bytes 221216 | tf_op jit(solution)/shard_map/ppermute | solution.py:40
  68.5 0.0 collective-permute-done.8.refs_2_
  68.6 2.6 %collective-permute-done.7.refs_1_ = bf16[144,768]{1,0:T(8,128)(2,1)S(1)} collective-permute-done((bf16[144,768]{1,0:T(8,128)(2,1)S(1)}, bf16[144,768]{1,0:T(8,128)(2,1)S(1)}, u32[]{:S(2)}, u32[]{:S(2)}) %collective-permute-start.7) | collective-permute-done | bytes 221216 | tf_op jit(solution)/shard_map/ppermute | solution.py:40
  71.1 0.3 shard_map.56
  71.4 11.9 %all_to_all.11.heads_ref = bf16[8,96,128]{2,1,0:T(8,128)(2,1)S(1)} all-to-all(bf16[8,96,128]{2,1,0:T(8,128)(2,1)S(1)} %bitcast.56), channel_id=1, replica_groups=mesh['zl'=2,'core'=2,'zh'=4,'y'=4,'x'=4] {'zh','zl'}, dimensions={0} | all-to-all | bytes 393216 | tf_op jit(solution)/shard_map/all_to_all | solution.py:361
  83.3 0.0 collective-permute-done.10.beside_ref
  83.3 1.6 %shard_map.57 = bf16[96,4096]{1,0:T(8,128)(2,1)S(1)} custom-call(bf16[8,96,128]{2,1,0:T(8,128)(2,1)S(1)} %all_to_all.11.heads_ref, bf16[512,4096]{1,0:T(8,128)(2,1)S(1)} %copy-done, bf16[512,4096]{1,0:T(8,128)(2,1)S(1)} %collective-permute-done.10.beside_ref), custom_call_target="tpu_custom_call" | custom-call | tf_op jit(solution)/shard_map/pallas_call | solution.py:316
  85.0 4.8 %collective-permute-start.11 = (bf16[48,4096]{1,0:T(8,128)(2,1)S(1)}, bf16[48,4096]{1,0:T(8,128)(2,1)S(1)}, u32[]{:S(2)}, u32[]{:S(2)}) collective-permute-start(bf16[48,4096]{1,0:T(8,128)(2,1)S(1)} %slice.56), channel_id=1, source_target_pairs={{0,64},{64,0},{1,65},{65,1},{2,66},{66,2},{3,67},{67,3},{4,68},{68... | collective-permute-start | bytes 1179656 | tf_op jit(solution)/shard_map/ppermute | solution.py:40
  89.8 1.3 %collective-permute-done.11 = bf16[48,4096]{1,0:T(8,128)(2,1)S(1)} collective-permute-done((bf16[48,4096]{1,0:T(8,128)(2,1)S(1)}, bf16[48,4096]{1,0:T(8,128)(2,1)S(1)}, u32[]{:S(2)}, u32[]{:S(2)}) %collective-permute-start.11) | collective-permute-done | bytes 393248 | tf_op jit(solution)/shard_map/ppermute | solution.py:40
  91.2 0.8 fusion
  (21 shorter events, 0.4 us)
Async XLA Ops:
  0.0 32.2 %copy-start = (bf16[512,4096]{1,0:T(8,128)(2,1)S(1)}, bf16[512,4096]{1,0:T(8,128)(2,1)}, u32[]{:S(2)}) copy-start(bf16[512,4096]{1,0:T(8,128)(2,1)} %own_ref.1) | copy-start | bytes 12582916
  2.6 4.5 %collective-permute-start = (bf16[8,3,48,128]{3,2,0,1:T(8,128)(2,1)S(1)}, bf16[8,3,48,128]{3,2,0,1:T(8,128)(2,1)S(1)}, u32[]{:S(2)}, u32[]{:S(2)}) collective-permute-start(bf16[8,3,48,128]{3,2,0,1:T(8,128)(2,1)S(1)} %pad_maximum_fusion.1), channel_id=1, source_target_pairs={{0,64},{64,0},{1,65},{65,1},{2,66},{66,2},{3,67},{67,3},{4,68},{68... | collective-permute-start | bytes 884744 | tf_op jit(solution)/shard_map/ppermute | solution.py:40
  32.2 51.1 %collective-permute-start.10 = (bf16[512,4096]{1,0:T(8,128)(2,1)S(1)}, bf16[512,4096]{1,0:T(8,128)(2,1)S(1)}, u32[]{:S(2)}, u32[]{:S(2)}) collective-permute-start(bf16[512,4096]{1,0:T(8,128)(2,1)S(1)} %copy-done), channel_id=1, source_target_pairs={{0,128},{16,144},{32,160},{48,176},{64,240},{80,192},{96,208},{112... | collective-permute-start | bytes 12582920 | tf_op jit(solution)/shard_map/ppermute | solution.py:40
  32.3 7.6 %collective-permute-start.4 = (bf16[8,208,128]{2,1,0:T(8,128)(2,1)S(1)}, bf16[8,208,128]{2,1,0:T(8,128)(2,1)S(1)}, u32[]{:S(2)}, u32[]{:S(2)}) collective-permute-start(bf16[8,208,128]{2,1,0:T(8,128)(2,1)S(1)} %pad_maximum_fusion.refs_4_), channel_id=1, source_target_pairs={{0,12},{1,13},{2,14},{3,15},{4,0},{5,1},{6,2},{7,3},{8,4},{9,5},{1... | collective-permute-start | bytes 1277960 | tf_op jit(solution)/shard_map/ppermute | solution.py:40
  34.9 11.2 %collective-permute-start.2 = (bf16[8,112,128]{2,1,0:T(8,128)(2,1)S(1)}, bf16[8,112,128]{2,1,0:T(8,128)(2,1)S(1)}, u32[]{:S(2)}, u32[]{:S(2)}) collective-permute-start(bf16[8,112,128]{2,1,0:T(8,128)(2,1)S(1)} %pad_maximum_fusion.2.refs_0_), channel_id=1, source_target_pairs={{0,1},{1,2},{2,3},{3,0},{4,5},{5,6},{6,7},{7,4},{8,9},{9,10},{10,1... | collective-permute-start | bytes 688136 | tf_op jit(solution)/shard_map/ppermute | solution.py:40
  36.2 14.4 %collective-permute-start.6 = (bf16[8,208,128]{2,1,0:T(8,128)(2,1)S(1)}, bf16[8,208,128]{2,1,0:T(8,128)(2,1)S(1)}, u32[]{:S(2)}, u32[]{:S(2)}) collective-permute-start(bf16[8,208,128]{2,1,0:T(8,128)(2,1)S(1)} %pad_maximum_fusion.refs_4_), channel_id=1, source_target_pairs={{0,4},{1,5},{2,6},{3,7},{4,8},{5,9},{6,10},{7,11},{8,12},{9,13},{1... | collective-permute-start | bytes 1277960 | tf_op jit(solution)/shard_map/ppermute | solution.py:40
  39.9 12.5 %collective-permute-start.5 = (bf16[8,208,128]{2,1,0:T(8,128)(2,1)S(1)}, bf16[8,208,128]{2,1,0:T(8,128)(2,1)S(1)}, u32[]{:S(2)}, u32[]{:S(2)}) collective-permute-start(bf16[8,208,128]{2,1,0:T(8,128)(2,1)S(1)} %collective-permute-done.4.refs_5_), channel_id=1, source_target_pairs={{0,12},{1,13},{2,14},{3,15},{4,0},{5,1},{6,2},{7,3},{8,4},{9,5},{1... | collective-permute-start | bytes 1277960 | tf_op jit(solution)/shard_map/ppermute | solution.py:40
  43.3 7.3 %collective-permute-start.1 = (bf16[8,112,128]{2,1,0:T(8,128)(2,1)S(1)}, bf16[8,112,128]{2,1,0:T(8,128)(2,1)S(1)}, u32[]{:S(2)}, u32[]{:S(2)}) collective-permute-start(bf16[8,112,128]{2,1,0:T(8,128)(2,1)S(1)} %pad_maximum_fusion.2.refs_0_), channel_id=1, source_target_pairs={{0,3},{1,0},{2,1},{3,2},{4,7},{5,4},{6,5},{7,6},{8,11},{9,8},{10,9... | collective-permute-start | bytes 688136 | tf_op jit(solution)/shard_map/ppermute | solution.py:40
  46.0 6.4 %collective-permute-start.3 = (bf16[8,112,128]{2,1,0:T(8,128)(2,1)S(1)}, bf16[8,112,128]{2,1,0:T(8,128)(2,1)S(1)}, u32[]{:S(2)}, u32[]{:S(2)}) collective-permute-start(bf16[8,112,128]{2,1,0:T(8,128)(2,1)S(1)} %collective-permute-done.2.refs_3_), channel_id=1, source_target_pairs={{0,1},{1,2},{2,3},{3,0},{4,5},{5,6},{6,7},{7,4},{8,9},{9,10},{10,1... | collective-permute-start | bytes 688136 | tf_op jit(solution)/shard_map/ppermute | solution.py:40
  62.1 6.5 %collective-permute-start.9 = (bf16[144,768]{1,0:T(8,128)(2,1)S(1)}, bf16[144,768]{1,0:T(8,128)(2,1)S(1)}, u32[]{:S(2)}, u32[]{:S(2)}) collective-permute-start(bf16[144,768]{1,0:T(8,128)(2,1)S(1)} %get-tuple-element.9), channel_id=1, source_target_pairs={{0,2},{1,3},{2,0},{3,1},{4,6},{5,7},{6,4},{7,5},{8,10},{9,11},{10,... | collective-permute-start | bytes 663560 | tf_op jit(solution)/shard_map/ppermute | solution.py:40
  62.2 6.4 %collective-permute-start.8 = (bf16[144,768]{1,0:T(8,128)(2,1)S(1)}, bf16[144,768]{1,0:T(8,128)(2,1)S(1)}, u32[]{:S(2)}, u32[]{:S(2)}) collective-permute-start(bf16[144,768]{1,0:T(8,128)(2,1)S(1)} %get-tuple-element.10), channel_id=1, source_target_pairs={{0,3},{1,0},{2,1},{3,2},{4,7},{5,4},{6,5},{7,6},{8,11},{9,8},{10,9... | collective-permute-start | bytes 663560 | tf_op jit(solution)/shard_map/ppermute | solution.py:40
  63.6 7.5 %collective-permute-start.7 = (bf16[144,768]{1,0:T(8,128)(2,1)S(1)}, bf16[144,768]{1,0:T(8,128)(2,1)S(1)}, u32[]{:S(2)}, u32[]{:S(2)}) collective-permute-start(bf16[144,768]{1,0:T(8,128)(2,1)S(1)} %get-tuple-element.11), channel_id=1, source_target_pairs={{0,1},{1,2},{2,3},{3,0},{4,5},{5,6},{6,7},{7,4},{8,9},{9,10},{10,1... | collective-permute-start | bytes 663560 | tf_op jit(solution)/shard_map/ppermute | solution.py:40
  85.0 6.2 %collective-permute-start.11 = (bf16[48,4096]{1,0:T(8,128)(2,1)S(1)}, bf16[48,4096]{1,0:T(8,128)(2,1)S(1)}, u32[]{:S(2)}, u32[]{:S(2)}) collective-permute-start(bf16[48,4096]{1,0:T(8,128)(2,1)S(1)} %slice.56), channel_id=1, source_target_pairs={{0,64},{64,0},{1,65},{65,1},{2,66},{66,2},{3,67},{67,3},{4,68},{68... | collective-permute-start | bytes 1179656 | tf_op jit(solution)/shard_map/ppermute | solution.py:40

commit v4 on v3

--- a/solution.py
+++ b/solution.py
@@ -247,7 +247,7 @@
 
 
 def project_kernel(heads_ref, own_ref, beside_ref, out_ref, held):
-    zl, tile = at_spot()[0], 2048
+    zl, tile = at_spot()[0], 4096
     for zh in range(4):
         columns = slice(zh * HD, (zh + 1) * HD)
         held[0, :, columns] = heads_ref[2 * zh + zl]
@@ -319,7 +319,7 @@
         in_specs=vmem(3),
         out_specs=vmem(1)[0],
         scratch_shapes=[pltpu.VMEM((2, PART, 4 * HD), jnp.bfloat16)],
-        compiler_params=pltpu.CompilerParams(vmem_limit_bytes=10 * 1024 * 1024),
+        compiler_params=pltpu.CompilerParams(vmem_limit_bytes=14 * 1024 * 1024),
     )(heads, own, beside)
 
 
@@ -344,7 +344,7 @@
     held, weight = lax.optimization_barrier((held, out_weight))
 
     def next_chip(at):
-        z = (2 * at["zh"] + at["zl"] + (1 if at["core"] == 0 else -1)) % 8
+        z = (2 * at["zh"] + at["zl"] + (1 if at["core"] == 1 else -1)) % 8
         return {"zh": z // 2, "zl": z % 2}
 
     beside = permute(weight, ("zl", "core", "zh"), next_chip)

time: 92.9 us -> 91.7 us (0.987)
  waiting for transfers between devices: 19.1 us -> 17.4 us
  blocking collectives: 36.8 us -> 37.8 us
    ppermute x12, waiting for transfers between devices: 19.1 us -> 17.4 us  [permute(): return lax.ppermute(array, tuple(axes), pairs)]
    all_to_all x1, blocking collectives: 11.9 us -> 12.9 us  [body(): heads = lax.all_to_all(attended, ('zh', 'zl'), 0, 0, tiled=True)]
where the time goes in v4:
time: 91.7 us; the launch traced here: 91.6 us
  blocking collectives  37.8 us (41%)
  starting transfers between devices  20.3 us (22%)
  waiting for transfers between devices  17.4 us (19%)
  Pallas kernels  11.3 us (12%)
  local copies, waits for them, and re-layouts  2.83 us (3%)
  other arithmetic  1.73 us (2%)
    all_to_all x1, blocking collectives, body(): held = lax.all_to_all(sent, ('zh', 'zl'), 0, 0, tiled=True)  24.9 us
    ppermute x12, starting transfers between devices, permute(): return lax.ppermute(array, tuple(axes), pairs)  20.3 us
    ppermute x12, waiting for transfers between devices, permute(): return lax.ppermute(array, tuple(axes), pairs)  17.4 us
    all_to_all x1, blocking collectives, body(): heads = lax.all_to_all(attended, ('zh', 'zl'), 0, 0, tiled=True)  12.9 us
    pallas_call x1, Pallas kernels, attend(): pl.pallas_call(attention_kernel, out_shape=jax.ShapeDtypeStruct((4, HD +...  9.56 us
    dynamic_slice x8, local copies, waits for them, and re-layouts, heads_of(): array = lax.dynamic_index_in_dim(array, c, 2, keepdims=False)  2.59 us
  transfers between devices with their start and end apart: 12, of which 7 were waited for; matrix products, arithmetic and copies ran while one was open for 1% of the time, Pallas kernels for 11%

profile of v4, /device:TPU:1, one launch (start us, length us, event | category | flops | bytes accessed | tf_op | source)
XLA Modules:
  0.0 91.6 jit_solution(12290769856346617683)
XLA Ops:
  0.0 0.0 copy-start
  0.0 1.2 %constant_dynamic-slice_fusion.4 = (bf16[48,2,1,4,128]{4,3,2,1,0:T(4,128)(2,1)S(1)}, bf16[48,2,1,4,128]{4,3,2,1,0:T(4,128)(2,1)S(1)}) fusion(bf16[48,2,2,4,128]{4,3,2,1,0:T(4,128)(2,1)} %bitcast.63, s32[]{:T(128)S(6)} %select_n.12, s32[]{:T(128)S(6)} %select_n.11), kind=kLoop, calls=%fused_computation.25 | loop fusion | bytes 393224 | tf_op jit(solution)/shard_map/jit(dynamic_index_in_dim)/dynamic_slice | solution.py:331
  1.2 1.3 %constant_dynamic-slice_fusion = (bf16[48,2,1,4,128]{4,3,2,1,0:T(4,128)(2,1)S(1)}, bf16[48,2,1,4,128]{4,3,2,1,0:T(4,128)(2,1)S(1)}, bf16[48,2,1,4,128]{4,3,2,1,0:T(4,128)(2,1)S(1)}, bf16[48,2,1,4,128]{4,3,2,1,0:T(4,128)(2,1)S(1)}) fusion(bf16[48,2,2,4,128]{4,3,2,1,0:T(4,128)(2,1)} %bitcast.64, s32[]{:T(128)S(6)} %select_n.11, s32[]{:T(128)S(6)} %select_n.12, ...), kind=kLoop, calls=%fused_computation.21 | loop fusion | bytes 786440 | tf_op jit(solution)/shard_map/jit(dynamic_index_in_dim)/dynamic_slice | solution.py:331
  2.6 3.3 %collective-permute-start = (bf16[8,3,48,128]{3,2,0,1:T(8,128)(2,1)S(1)}, bf16[8,3,48,128]{3,2,0,1:T(8,128)(2,1)S(1)}, u32[]{:S(2)}, u32[]{:S(2)}) collective-permute-start(bf16[8,3,48,128]{3,2,0,1:T(8,128)(2,1)S(1)} %pad_maximum_fusion.1), channel_id=1, source_target_pairs={{0,64},{64,0},{1,65},{65,1},{2,66},{66,2},{3,67},{67,3},{4,68},{68... | collective-permute-start | bytes 884744 | tf_op jit(solution)/shard_map/ppermute | solution.py:40
  6.0 0.8 convert_reduce_fusion
  6.8 0.3 collective-permute-done
  7.3 24.9 %all_to_all.10 = bf16[8,296,128]{2,1,0:T(8,128)(2,1)S(1)} all-to-all(bf16[8,296,128]{2,1,0:T(8,128)(2,1)S(1)} %constant_dynamic-update-slice_fusion), channel_id=1, replica_groups=mesh['zl'=2,'core'=2,'zh'=4,'y'=4,'x'=4] {'zh','zl'}, dimensions={0} | all-to-all | bytes 1212416 | tf_op jit(solution)/shard_map/all_to_all | solution.py:343
  32.2 0.0 copy-done
  32.2 0.0 collective-permute-start.10
  32.3 2.6 %collective-permute-start.4 = (bf16[8,208,128]{2,1,0:T(8,128)(2,1)S(1)}, bf16[8,208,128]{2,1,0:T(8,128)(2,1)S(1)}, u32[]{:S(2)}, u32[]{:S(2)}) collective-permute-start(bf16[8,208,128]{2,1,0:T(8,128)(2,1)S(1)} %pad_maximum_fusion.refs_4_), channel_id=1, source_target_pairs={{0,12},{1,13},{2,14},{3,15},{4,0},{5,1},{6,2},{7,3},{8,4},{9,5},{1... | collective-permute-start | bytes 1277960 | tf_op jit(solution)/shard_map/ppermute | solution.py:40
  34.9 1.4 %collective-permute-start.2 = (bf16[8,112,128]{2,1,0:T(8,128)(2,1)S(1)}, bf16[8,112,128]{2,1,0:T(8,128)(2,1)S(1)}, u32[]{:S(2)}, u32[]{:S(2)}) collective-permute-start(bf16[8,112,128]{2,1,0:T(8,128)(2,1)S(1)} %pad_maximum_fusion.2.refs_0_), channel_id=1, source_target_pairs={{0,1},{1,2},{2,3},{3,0},{4,5},{5,6},{6,7},{7,4},{8,9},{9,10},{10,1... | collective-permute-start | bytes 688136 | tf_op jit(solution)/shard_map/ppermute | solution.py:40
  36.2 0.0 collective-permute-start.6
  36.2 3.7 %collective-permute-done.4.refs_5_ = bf16[8,208,128]{2,1,0:T(8,128)(2,1)S(1)} collective-permute-done((bf16[8,208,128]{2,1,0:T(8,128)(2,1)S(1)}, bf16[8,208,128]{2,1,0:T(8,128)(2,1)S(1)}, u32[]{:S(2)}, u32[]{:S(2)}) %collective-permute-start.4) | collective-permute-done | bytes 426016 | tf_op jit(solution)/shard_map/ppermute | solution.py:40
  39.9 3.1 %collective-permute-start.5 = (bf16[8,208,128]{2,1,0:T(8,128)(2,1)S(1)}, bf16[8,208,128]{2,1,0:T(8,128)(2,1)S(1)}, u32[]{:S(2)}, u32[]{:S(2)}) collective-permute-start(bf16[8,208,128]{2,1,0:T(8,128)(2,1)S(1)} %collective-permute-done.4.refs_5_), channel_id=1, source_target_pairs={{0,12},{1,13},{2,14},{3,15},{4,0},{5,1},{6,2},{7,3},{8,4},{9,5},{1... | collective-permute-start | bytes 1277960 | tf_op jit(solution)/shard_map/ppermute | solution.py:40
  43.0 3.0 %collective-permute-start.1 = (bf16[8,112,128]{2,1,0:T(8,128)(2,1)S(1)}, bf16[8,112,128]{2,1,0:T(8,128)(2,1)S(1)}, u32[]{:S(2)}, u32[]{:S(2)}) collective-permute-start(bf16[8,112,128]{2,1,0:T(8,128)(2,1)S(1)} %pad_maximum_fusion.2.refs_0_), channel_id=1, source_target_pairs={{0,3},{1,0},{2,1},{3,2},{4,7},{5,4},{6,5},{7,6},{8,11},{9,8},{10,9... | collective-permute-start | bytes 688136 | tf_op jit(solution)/shard_map/ppermute | solution.py:40
  46.0 0.0 collective-permute-done.2.refs_3_
  46.0 0.0 collective-permute-start.3
  46.0 5.1 %collective-permute-done.1.refs_1_ = bf16[8,112,128]{2,1,0:T(8,128)(2,1)S(1)} collective-permute-done((bf16[8,112,128]{2,1,0:T(8,128)(2,1)S(1)}, bf16[8,112,128]{2,1,0:T(8,128)(2,1)S(1)}, u32[]{:S(2)}, u32[]{:S(2)}) %collective-permute-start.1) | collective-permute-done | bytes 229408 | tf_op jit(solution)/shard_map/ppermute | solution.py:40
  51.1 0.0 collective-permute-done.6.refs_7_
  51.1 1.0 %collective-permute-done.3.refs_2_ = bf16[8,112,128]{2,1,0:T(8,128)(2,1)S(1)} collective-permute-done((bf16[8,112,128]{2,1,0:T(8,128)(2,1)S(1)}, bf16[8,112,128]{2,1,0:T(8,128)(2,1)S(1)}, u32[]{:S(2)}, u32[]{:S(2)}) %collective-permute-start.3) | collective-permute-done | bytes 229408 | tf_op jit(solution)/shard_map/ppermute | solution.py:40
  52.1 0.0 collective-permute-done.5.refs_6_
  52.1 9.6 %shard_map.55 = bf16[4,144,768]{2,1,0:T(8,128)(2,1)S(1)} custom-call(bf16[8,112,128]{2,1,0:T(8,128)(2,1)S(1)} %pad_maximum_fusion.2.refs_0_, bf16[8,112,128]{2,1,0:T(8,128)(2,1)S(1)} %collective-permute-done.1.refs_1_, bf16[8,112,128]{2,1,0:T(8,128)(2,1)S(1)} %collective-permute-done.3.refs_2_, bf16[8,112,128]{2,1,0:T(8,128)(2,1)S(1)} %collective-permute-done.2.refs_3_, ...), custom_call_target="tpu_custom_call" | custom-call | tf_op jit(solution)/shard_map/pallas_call | solution.py:273
  61.7 0.1 slice_bitcast_fusion
  61.8 0.1 collective-permute-start.9
  61.9 2.6 %collective-permute-start.8 = (bf16[144,768]{1,0:T(8,128)(2,1)S(1)}, bf16[144,768]{1,0:T(8,128)(2,1)S(1)}, u32[]{:S(2)}, u32[]{:S(2)}) collective-permute-start(bf16[144,768]{1,0:T(8,128)(2,1)S(1)} %get-tuple-element.10), channel_id=1, source_target_pairs={{0,3},{1,0},{2,1},{3,2},{4,7},{5,4},{6,5},{7,6},{8,11},{9,8},{10,9... | collective-permute-start | bytes 663560 | tf_op jit(solution)/shard_map/ppermute | solution.py:40
  64.4 0.5 collective-permute-start.7
  64.9 3.2 %collective-permute-done.9.refs_3_ = bf16[144,768]{1,0:T(8,128)(2,1)S(1)} collective-permute-done((bf16[144,768]{1,0:T(8,128)(2,1)S(1)}, bf16[144,768]{1,0:T(8,128)(2,1)S(1)}, u32[]{:S(2)}, u32[]{:S(2)}) %collective-permute-start.9) | collective-permute-done | bytes 221216 | tf_op jit(solution)/shard_map/ppermute | solution.py:40
  68.1 2.8 %collective-permute-done.8.refs_2_ = bf16[144,768]{1,0:T(8,128)(2,1)S(1)} collective-permute-done((bf16[144,768]{1,0:T(8,128)(2,1)S(1)}, bf16[144,768]{1,0:T(8,128)(2,1)S(1)}, u32[]{:S(2)}, u32[]{:S(2)}) %collective-permute-start.8) | collective-permute-done | bytes 221216 | tf_op jit(solution)/shard_map/ppermute | solution.py:40
  70.9 0.0 collective-permute-done.7.refs_1_
  70.9 0.3 shard_map.56
  71.2 12.9 %all_to_all.11.heads_ref = bf16[8,96,128]{2,1,0:T(8,128)(2,1)S(1)} all-to-all(bf16[8,96,128]{2,1,0:T(8,128)(2,1)S(1)} %bitcast.56), channel_id=1, replica_groups=mesh['zl'=2,'core'=2,'zh'=4,'y'=4,'x'=4] {'zh','zl'}, dimensions={0} | all-to-all | bytes 393216 | tf_op jit(solution)/shard_map/all_to_all | solution.py:361
  84.1 0.0 collective-permute-done.10.beside_ref
  84.1 1.5 %shard_map.57 = bf16[96,4096]{1,0:T(8,128)(2,1)S(1)} custom-call(bf16[8,96,128]{2,1,0:T(8,128)(2,1)S(1)} %all_to_all.11.heads_ref, bf16[512,4096]{1,0:T(8,128)(2,1)S(1)} %copy-done, bf16[512,4096]{1,0:T(8,128)(2,1)S(1)} %collective-permute-done.10.beside_ref), custom_call_target="tpu_custom_call" | custom-call | tf_op jit(solution)/shard_map/pallas_call | solution.py:316
  85.6 3.8 %collective-permute-start.11 = (bf16[48,4096]{1,0:T(8,128)(2,1)S(1)}, bf16[48,4096]{1,0:T(8,128)(2,1)S(1)}, u32[]{:S(2)}, u32[]{:S(2)}) collective-permute-start(bf16[48,4096]{1,0:T(8,128)(2,1)S(1)} %slice.56), channel_id=1, source_target_pairs={{0,64},{64,0},{1,65},{65,1},{2,66},{66,2},{3,67},{67,3},{4,68},{68... | collective-permute-start | bytes 1179656 | tf_op jit(solution)/shard_map/ppermute | solution.py:40
  89.4 1.3 %collective-permute-done.11 = bf16[48,4096]{1,0:T(8,128)(2,1)S(1)} collective-permute-done((bf16[48,4096]{1,0:T(8,128)(2,1)S(1)}, bf16[48,4096]{1,0:T(8,128)(2,1)S(1)}, u32[]{:S(2)}, u32[]{:S(2)}) %collective-permute-start.11) | collective-permute-done | bytes 393248 | tf_op jit(solution)/shard_map/ppermute | solution.py:40
  90.7 0.8 fusion
  (21 shorter events, 0.4 us)
Async XLA Ops:
  0.0 32.2 %copy-start = (bf16[512,4096]{1,0:T(8,128)(2,1)S(1)}, bf16[512,4096]{1,0:T(8,128)(2,1)}, u32[]{:S(2)}) copy-start(bf16[512,4096]{1,0:T(8,128)(2,1)} %own_ref.1) | copy-start | bytes 12582916
  2.6 4.5 %collective-permute-start = (bf16[8,3,48,128]{3,2,0,1:T(8,128)(2,1)S(1)}, bf16[8,3,48,128]{3,2,0,1:T(8,128)(2,1)S(1)}, u32[]{:S(2)}, u32[]{:S(2)}) collective-permute-start(bf16[8,3,48,128]{3,2,0,1:T(8,128)(2,1)S(1)} %pad_maximum_fusion.1), channel_id=1, source_target_pairs={{0,64},{64,0},{1,65},{65,1},{2,66},{66,2},{3,67},{67,3},{4,68},{68... | collective-permute-start | bytes 884744 | tf_op jit(solution)/shard_map/ppermute | solution.py:40
  32.2 51.9 %collective-permute-start.10 = (bf16[512,4096]{1,0:T(8,128)(2,1)S(1)}, bf16[512,4096]{1,0:T(8,128)(2,1)S(1)}, u32[]{:S(2)}, u32[]{:S(2)}) collective-permute-start(bf16[512,4096]{1,0:T(8,128)(2,1)S(1)} %copy-done), channel_id=1, source_target_pairs={{0,176},{16,128},{32,144},{48,160},{64,192},{80,208},{96,224},{112... | collective-permute-start | bytes 12582920 | tf_op jit(solution)/shard_map/ppermute | solution.py:40
  32.3 7.6 %collective-permute-start.4 = (bf16[8,208,128]{2,1,0:T(8,128)(2,1)S(1)}, bf16[8,208,128]{2,1,0:T(8,128)(2,1)S(1)}, u32[]{:S(2)}, u32[]{:S(2)}) collective-permute-start(bf16[8,208,128]{2,1,0:T(8,128)(2,1)S(1)} %pad_maximum_fusion.refs_4_), channel_id=1, source_target_pairs={{0,12},{1,13},{2,14},{3,15},{4,0},{5,1},{6,2},{7,3},{8,4},{9,5},{1... | collective-permute-start | bytes 1277960 | tf_op jit(solution)/shard_map/ppermute | solution.py:40
  34.9 11.2 %collective-permute-start.2 = (bf16[8,112,128]{2,1,0:T(8,128)(2,1)S(1)}, bf16[8,112,128]{2,1,0:T(8,128)(2,1)S(1)}, u32[]{:S(2)}, u32[]{:S(2)}) collective-permute-start(bf16[8,112,128]{2,1,0:T(8,128)(2,1)S(1)} %pad_maximum_fusion.2.refs_0_), channel_id=1, source_target_pairs={{0,1},{1,2},{2,3},{3,0},{4,5},{5,6},{6,7},{7,4},{8,9},{9,10},{10,1... | collective-permute-start | bytes 688136 | tf_op jit(solution)/shard_map/ppermute | solution.py:40
  36.2 14.9 %collective-permute-start.6 = (bf16[8,208,128]{2,1,0:T(8,128)(2,1)S(1)}, bf16[8,208,128]{2,1,0:T(8,128)(2,1)S(1)}, u32[]{:S(2)}, u32[]{:S(2)}) collective-permute-start(bf16[8,208,128]{2,1,0:T(8,128)(2,1)S(1)} %pad_maximum_fusion.refs_4_), channel_id=1, source_target_pairs={{0,4},{1,5},{2,6},{3,7},{4,8},{5,9},{6,10},{7,11},{8,12},{9,13},{1... | collective-permute-start | bytes 1277960 | tf_op jit(solution)/shard_map/ppermute | solution.py:40
  39.9 12.2 %collective-permute-start.5 = (bf16[8,208,128]{2,1,0:T(8,128)(2,1)S(1)}, bf16[8,208,128]{2,1,0:T(8,128)(2,1)S(1)}, u32[]{:S(2)}, u32[]{:S(2)}) collective-permute-start(bf16[8,208,128]{2,1,0:T(8,128)(2,1)S(1)} %collective-permute-done.4.refs_5_), channel_id=1, source_target_pairs={{0,12},{1,13},{2,14},{3,15},{4,0},{5,1},{6,2},{7,3},{8,4},{9,5},{1... | collective-permute-start | bytes 1277960 | tf_op jit(solution)/shard_map/ppermute | solution.py:40
  43.0 8.1 %collective-permute-start.1 = (bf16[8,112,128]{2,1,0:T(8,128)(2,1)S(1)}, bf16[8,112,128]{2,1,0:T(8,128)(2,1)S(1)}, u32[]{:S(2)}, u32[]{:S(2)}) collective-permute-start(bf16[8,112,128]{2,1,0:T(8,128)(2,1)S(1)} %pad_maximum_fusion.2.refs_0_), channel_id=1, source_target_pairs={{0,3},{1,0},{2,1},{3,2},{4,7},{5,4},{6,5},{7,6},{8,11},{9,8},{10,9... | collective-permute-start | bytes 688136 | tf_op jit(solution)/shard_map/ppermute | solution.py:40
  46.0 6.1 %collective-permute-start.3 = (bf16[8,112,128]{2,1,0:T(8,128)(2,1)S(1)}, bf16[8,112,128]{2,1,0:T(8,128)(2,1)S(1)}, u32[]{:S(2)}, u32[]{:S(2)}) collective-permute-start(bf16[8,112,128]{2,1,0:T(8,128)(2,1)S(1)} %collective-permute-done.2.refs_3_), channel_id=1, source_target_pairs={{0,1},{1,2},{2,3},{3,0},{4,5},{5,6},{6,7},{7,4},{8,9},{9,10},{10,1... | collective-permute-start | bytes 688136 | tf_op jit(solution)/shard_map/ppermute | solution.py:40
  61.8 6.4 %collective-permute-start.9 = (bf16[144,768]{1,0:T(8,128)(2,1)S(1)}, bf16[144,768]{1,0:T(8,128)(2,1)S(1)}, u32[]{:S(2)}, u32[]{:S(2)}) collective-permute-start(bf16[144,768]{1,0:T(8,128)(2,1)S(1)} %get-tuple-element.9), channel_id=1, source_target_pairs={{0,2},{1,3},{2,0},{3,1},{4,6},{5,7},{6,4},{7,5},{8,10},{9,11},{10,... | collective-permute-start | bytes 663560 | tf_op jit(solution)/shard_map/ppermute | solution.py:40
  61.9 9.1 %collective-permute-start.8 = (bf16[144,768]{1,0:T(8,128)(2,1)S(1)}, bf16[144,768]{1,0:T(8,128)(2,1)S(1)}, u32[]{:S(2)}, u32[]{:S(2)}) collective-permute-start(bf16[144,768]{1,0:T(8,128)(2,1)S(1)} %get-tuple-element.10), channel_id=1, source_target_pairs={{0,3},{1,0},{2,1},{3,2},{4,7},{5,4},{6,5},{7,6},{8,11},{9,8},{10,9... | collective-permute-start | bytes 663560 | tf_op jit(solution)/shard_map/ppermute | solution.py:40
  64.4 6.5 %collective-permute-start.7 = (bf16[144,768]{1,0:T(8,128)(2,1)S(1)}, bf16[144,768]{1,0:T(8,128)(2,1)S(1)}, u32[]{:S(2)}, u32[]{:S(2)}) collective-permute-start(bf16[144,768]{1,0:T(8,128)(2,1)S(1)} %get-tuple-element.11), channel_id=1, source_target_pairs={{0,1},{1,2},{2,3},{3,0},{4,5},{5,6},{6,7},{7,4},{8,9},{9,10},{10,1... | collective-permute-start | bytes 663560 | tf_op jit(solution)/shard_map/ppermute | solution.py:40
  85.6 5.1 %collective-permute-start.11 = (bf16[48,4096]{1,0:T(8,128)(2,1)S(1)}, bf16[48,4096]{1,0:T(8,128)(2,1)S(1)}, u32[]{:S(2)}, u32[]{:S(2)}) collective-permute-start(bf16[48,4096]{1,0:T(8,128)(2,1)S(1)} %slice.56), channel_id=1, source_target_pairs={{0,64},{64,0},{1,65},{65,1},{2,66},{66,2},{3,67},{67,3},{4,68},{68... | collective-permute-start | bytes 1179656 | tf_op jit(solution)/shard_map/ppermute | solution.py:40
